TPU v7x, 32 devices: a whole 2x2x4 slice. The times are simulated.
32 devices in a mesh: dp: 4 (over y, core), owner: 8 (over z, x).
Axes of the slice: x: 2, y: 2, z: 4, core: 2. Of those that a mesh axis runs over, the one named last changes fastest.
Arguments:
- tokens: bfloat16 [2048, 4096], P('dp'), may hold values from -6 to 6
- route: int32 [2048, 1], P('dp'), may hold values from 0 to 3; in each aligned block of 512 rows (0 to 511, 512 to 1023, ...) at most 384 rows name the same one
- gate_prob: float32 [2048], P('dp'), may hold values from 0.1 to 1
- w_gate: bfloat16 [4096, 6144], P('dp', 'owner'), may hold values from -0.09375 to 0.09375
- w_up: bfloat16 [4096, 6144], P('dp', 'owner'), may hold values from -0.09375 to 0.09375
- w_down: bfloat16 [6144, 4096], P('owner', 'dp'), may hold values from -0.15625 to 0.15625
- d_out: bfloat16 [2048, 4096], P('dp', 'owner'), may hold values from -1.5 to 1.5
Outputs:
- mixed: bfloat16 [2048, 4096], P('dp', 'owner')
- grad_tokens: bfloat16 [2048, 4096], P('dp', 'owner')
- grad_gate: float32 [2048], P('dp')
- grad_w_gate: float32 [4096, 6144], P('dp', 'owner')
- grad_w_up: float32 [4096, 6144], P('dp', 'owner')
- grad_w_down: float32 [6144, 4096], P('owner', 'dp')
Inputs may be any that keep to these rules, and one draw needn't show every extreme that they name: `route`: in every aligned block of 512 rows no expert is named by more than 384 rows, and in some block one expert is named by exactly 384 rows.
All inputs are finite; a program needn't handle non-finite values.
Results may differ from a plain program's by a relative error of at most 0.017.
Values may be sent and summed in bfloat16 or wider, within the bound.
No kernel may reach another device: no remote copies, remote signals or barrier semaphores. Data moves between devices by JAX's collectives and lax.ppermute only.
A program may use at most 128 MiB of HBM per device.

v0:
```python
import jax
import jax.numpy as jnp
from jax import lax
from jax.sharding import PartitionSpec as P

EXPERTS = 4


def contract_rows(left, right):
    return lax.dot_general(
        left, right, (((0,), (0,)), ((), ())), preferred_element_type=jnp.float32
    )


def contract_cols(left, right):
    return lax.dot_general(
        left, right, (((1,), (1,)), ((), ())), preferred_element_type=jnp.float32
    )


def local(tokens, route, gate_prob, w_gate, w_up, w_down, d_out):
    row_count = tokens.shape[0]
    capacity = 3 * row_count // 4
    pieces = lax.axis_size("owner") // EXPERTS
    expert = lax.axis_index("owner") // pieces
    full_gate, full_up, full_down = (
        lax.all_gather(w_gate, "dp", axis=0, tiled=True),
        lax.all_gather(w_up, "dp", axis=0, tiled=True),
        lax.all_gather(w_down, "dp", axis=1, tiled=True),
    )
    selected = route[:, 0] == expert
    slot_index = jnp.cumsum(selected.astype(jnp.int32)) - 1
    safe_index = jnp.maximum(slot_index, 0)
    slot_ids = jnp.arange(capacity, dtype=jnp.int32)
    one_hot = jnp.logical_and(slot_index[None, :] == slot_ids[:, None], selected[None, :])
    dispatch = one_hot.astype(jnp.bfloat16)
    slot_tokens = jnp.dot(dispatch, tokens, preferred_element_type=jnp.float32).astype(jnp.bfloat16)
    slot_probs = jnp.sum(jnp.where(one_hot, gate_prob[None, :], jnp.float32(0.0)), axis=1)
    row_weights = jnp.where(selected, gate_prob, jnp.float32(0.0))
    gate_pre = jnp.dot(slot_tokens, full_gate, preferred_element_type=jnp.float32)
    up_pre = jnp.dot(slot_tokens, full_up, preferred_element_type=jnp.float32)
    sigma = jax.nn.sigmoid(gate_pre)
    active = gate_pre * sigma
    hidden = (active * up_pre).astype(jnp.bfloat16)
    expert_out = jnp.dot(hidden, full_down, preferred_element_type=jnp.float32)
    row_terms = jnp.take(expert_out, safe_index, axis=0) * row_weights[:, None]
    mixed = lax.psum_scatter(
        row_terms.astype(jnp.bfloat16), "owner", scatter_dimension=1, tiled=True
    )
    d_full = lax.all_gather(d_out, "owner", axis=1, tiled=True)
    slot_cotangent = jnp.dot(dispatch, d_full, preferred_element_type=jnp.float32)
    slot_router = jnp.sum(slot_cotangent * expert_out, axis=1)
    router_terms = jnp.where(selected, jnp.take(slot_router, safe_index), jnp.float32(0.0))
    grad_gate = lax.psum(router_terms, "owner")
    d_expert = (slot_probs[:, None] * slot_cotangent).astype(jnp.bfloat16)
    d_hidden = contract_cols(d_expert, full_down)
    d_gate_pre = (d_hidden * up_pre * sigma * (1.0 + gate_pre * (1.0 - sigma))).astype(jnp.bfloat16)
    d_up_pre = (d_hidden * active).astype(jnp.bfloat16)
    slot_input = contract_cols(d_gate_pre, full_gate) + contract_cols(d_up_pre, full_up)
    input_terms = jnp.where(
        selected[:, None], jnp.take(slot_input, safe_index, axis=0), jnp.float32(0.0)
    )
    grad_tokens = lax.psum_scatter(
        input_terms.astype(jnp.bfloat16), "owner", scatter_dimension=1, tiled=True
    )
    gate_term = contract_rows(slot_tokens, d_gate_pre)
    up_term = contract_rows(slot_tokens, d_up_pre)
    down_term = contract_rows(hidden, d_expert)
    grad_w_gate, grad_w_up, grad_w_down = (
        lax.psum_scatter(
            gate_term.astype(jnp.bfloat16), "dp", scatter_dimension=0, tiled=True
        ).astype(jnp.float32),
        lax.psum_scatter(
            up_term.astype(jnp.bfloat16), "dp", scatter_dimension=0, tiled=True
        ).astype(jnp.float32),
        lax.psum_scatter(
            down_term.astype(jnp.bfloat16), "dp", scatter_dimension=1, tiled=True
        ).astype(jnp.float32),
    )
    return (mixed, grad_tokens, grad_gate, grad_w_gate, grad_w_up, grad_w_down)


def solution(mesh):
    in_specs = (
        P("dp", None),
        P("dp", None),
        P("dp"),
        P("dp", "owner"),
        P("dp", "owner"),
        P("owner", "dp"),
        P("dp", "owner"),
    )
    out_specs = (
        P("dp", "owner"),
        P("dp", "owner"),
        P("dp"),
        P("dp", "owner"),
        P("dp", "owner"),
        P("owner", "dp"),
    )
    return jax.shard_map(local, mesh=mesh, in_specs=in_specs, out_specs=out_specs, check_vma=False)
```

profile of v0, /device:TPU:0, one launch (start us, length us, event | category | flops | bytes accessed | tf_op | source)
XLA Modules:
  0.0 616.9 jit_solution(1215773136974058425)
XLA Ops:
  10.9 5.7 convolution_convert_fusion.3
  16.6 71.2 %all-gather.11.cloned.1.call-done = bf16[512,4096]{1,0:T(8,128)(2,1)} async-done(((bf16[512,512]{1,0:T(8,128)(2,1)}), bf16[512,4096]{1,0:T(8,128)(2,1)}) %all-gather.11.cloned.1.call-update) | async-done | bytes 4194320 | tf_op jit(solution)/shard_map/all_gather | solution.py:50
  87.8 6.6 %fusion.4 = f32[384,4096]{1,0:T(8,128)} fusion(bf16[512,4096]{1,0:T(8,128)(2,1)} %all-gather.11.cloned.1.call-done, s32[512]{0:T(512)S(1)} %get-tuple-element.10, pred[512]{0:T(512)(128)(4,1)S(1)} %get-tuple-element.14), kind=kOutput, calls=%fused_computation.22 | convolution fusion | flops 1611005952 | bytes 10488320 | tf_op jit(solution)/shard_map/dot_general | solution.py:51
  94.5 39.5 %all-gather.5.cloned.1.call-done = bf16[4096,768]{1,0:T(8,128)(2,1)} async-done(((bf16[1024,768]{1,0:T(8,128)(2,1)}), bf16[4096,768]{1,0:T(8,128)(2,1)}) %all-gather.5.cloned.1.call-update) | async-done | bytes 6291472 | tf_op jit(solution)/shard_map/all_gather | solution.py:27
  134.0 6.3 %fusion.14 = f32[384,768]{1,0:T(8,128)S(1)} fusion(bf16[384,4096]{1,0:T(8,128)(2,1)} %convolution_convert_fusion.3, bf16[4096,768]{1,0:T(8,128)(2,1)} %all-gather.5.cloned.1.call-done), kind=kOutput, calls=%fused_computation.40 | convolution fusion | flops 2415919104 | bytes 10616832 | tf_op jit(solution)/shard_map/dot_general | solution.py:40
  140.3 41.6 %all-gather.7.cloned.1.call-done = bf16[4096,768]{1,0:T(8,128)(2,1)} async-done(((bf16[1024,768]{1,0:T(8,128)(2,1)}), bf16[4096,768]{1,0:T(8,128)(2,1)}) %all-gather.7.cloned.1.call-update) | async-done | bytes 6291472 | tf_op jit(solution)/shard_map/all_gather | solution.py:28
  182.0 7.4 %fusion.15 = f32[384,768]{1,0:T(8,128)} fusion(bf16[384,4096]{1,0:T(8,128)(2,1)} %convolution_convert_fusion.3, bf16[4096,768]{1,0:T(8,128)(2,1)} %all-gather.7.cloned.1.call-done), kind=kOutput, calls=%fused_computation.41 | convolution fusion | flops 2415919104 | bytes 10616832 | tf_op jit(solution)/shard_map/dot_general | solution.py:41
  189.3 40.6 %all-gather.9.cloned.1.call-done = bf16[768,4096]{1,0:T(8,128)(2,1)} async-done(((bf16[768,1024]{1,0:T(8,128)(2,1)}), bf16[768,4096]{1,0:T(8,128)(2,1)}) %all-gather.9.cloned.1.call-update) | async-done | bytes 6291472 | tf_op jit(solution)/shard_map/all_gather | solution.py:29
  229.9 8.0 %multiply_convert_fusion.1 = (bf16[384,768]{1,0:T(8,128)(2,1)S(1)}, bf16[384,768]{1,0:T(8,128)(2,1)S(1)}, bf16[384,768]{1,0:T(8,128)(2,1)S(1)}) fusion(f32[384,768]{1,0:T(8,128)S(1)} %fusion.14, f32[384,768]{1,0:T(8,128)} %fusion.15, bf16[768,4096]{1,0:T(8,128)(2,1)} %all-gather.9.cloned.1.call-done, f32[384,4096]{1,0:T(8,128)} %fusion.4, ...), kind=kOutput, calls=%fused_computation.14 | convolution fusion | flops 2423488512 | bytes 16713216 | tf_op jit(solution)/shard_map/dot_general | solution.py:16
  238.7 5.6 convolution_convert_fusion
  244.4 8.1 %convolution_convert_fusion.2 = bf16[4096,768]{1,0:T(8,128)(2,1)} fusion(bf16[384,4096]{1,0:T(8,128)(2,1)} %convolution_convert_fusion.3, bf16[384,768]{1,0:T(8,128)(2,1)S(1)} %get-tuple-element.12), kind=kOutput, calls=%fused_computation.9 | convolution fusion | flops 2419064832 | bytes 10027008 | tf_op jit(solution)/shard_map/dot_general | solution.py:10
  252.6 8.8 %convolution_convert_fusion.1 = bf16[4096,768]{1,0:T(8,128)(2,1)} fusion(bf16[384,4096]{1,0:T(8,128)(2,1)} %convolution_convert_fusion.3, bf16[384,768]{1,0:T(8,128)(2,1)S(1)} %get-tuple-element.11), kind=kOutput, calls=%fused_computation.8 | convolution fusion | flops 2419064832 | bytes 10027008 | tf_op jit(solution)/shard_map/dot_general | solution.py:10
  261.5 5.0 fusion.16
  266.5 7.3 %convolution_add_fusion = bf16[384,4096]{1,0:T(8,128)(2,1)S(1)} fusion(f32[384,4096]{1,0:T(8,128)S(1)} %fusion.16, bf16[384,768]{1,0:T(8,128)(2,1)S(1)} %copy-done.5, bf16[4096,768]{1,0:T(8,128)(2,1)} %all-gather.7.cloned.1.call-done), kind=kOutput, calls=%fused_computation.12 | convolution fusion | flops 2419064832 | bytes 16318464 | tf_op jit(solution)/shard_map/dot_general | solution.py:16
  273.9 4.4 gather_fusion.2
  278.2 10.0 %multiply_reduce_fusion = (f32[384]{0:T(512)S(1)}, f32[384,4096]{1,0:T(8,128)}) fusion(f32[384,4096]{1,0:T(8,128)} %fusion.4, bf16[384,768]{1,0:T(8,128)(2,1)} %copy-done.1, bf16[768,4096]{1,0:T(8,128)(2,1)} %all-gather.9.cloned.1.call-done), kind=kOutput, calls=%fused_computation.10 | convolution fusion | flops 2419064320 | bytes 19465728 | tf_op jit(solution)/shard_map/dot_general | solution.py:45
  291.7 5.2 fusion
  297.0 11.6 %gather_fusion.1 = f32[512,4096]{1,0:T(8,128)} fusion(f32[384,4096]{1,0:T(8,128)} %get-tuple-element.18, s32[1024]{0:T(1024)S(1)} %pad_clamp_fusion.1), kind=kCustom, calls=%fused_computation.clone | custom fusion | bytes 16779264 | tf_op jit(solution)/shard_map/jit(_take)/gather | solution.py:46
  308.7 8.5 %fusion.1 = bf16[512,4096]{1,0:T(8,128)(2,1)} fusion(f32[512,4096]{1,0:T(8,128)} %gather_fusion.1, f32[512]{0:T(512)S(1)} %get-tuple-element.16, pred[512]{0:T(512)(128)(4,1)S(1)} %get-tuple-element.8), kind=kLoop, calls=%fused_computation.6 | loop fusion | flops 6291456 | bytes 12585472 | tf_op jit(solution)/shard_map/convert_element_type | solution.py:48
  317.2 22.3 %psum.7 = f32[512]{0:T(512)} all-reduce(f32[512]{0:T(512)S(1)} %get-tuple-element.7), channel_id=1, replica_groups=mesh['dp'=4,'owner'=8] {'owner'}, use_global_device_ids=true, to_apply=%region_6.8 | all-reduce | flops 512 | bytes 4096 | tf_op jit(solution)/shard_map/psum | solution.py:54
  342.9 20.9 %reduce-scatter.10.cloned.1.call-done = bf16[1024,768]{1,0:T(8,128)(2,1)} async-done(((bf16[4096,768]{1,0:T(8,128)(2,1)}), bf16[1024,768]{1,0:T(8,128)(2,1)}) %reduce-scatter.10.cloned.1.call-update) | async-done | bytes 1572880 | tf_op jit(solution)/shard_map/reduce_scatter | solution.py:70
  367.1 57.6 %reduce-scatter.12.cloned.1.call-done = bf16[1024,768]{1,0:T(8,128)(2,1)} async-done(((bf16[4096,768]{1,0:T(8,128)(2,1)}), bf16[1024,768]{1,0:T(8,128)(2,1)}) %reduce-scatter.12.cloned.1.call-update) | async-done | bytes 1572880 | tf_op jit(solution)/shard_map/reduce_scatter | solution.py:73
  428.1 89.8 %reduce-scatter.8.cloned.1.call-done = bf16[512,512]{1,0:T(8,128)(2,1)} async-done(((bf16[512,4096]{1,0:T(8,128)(2,1)}), bf16[512,512]{1,0:T(8,128)(2,1)}) %reduce-scatter.8.cloned.1.call-update) | async-done | bytes 524304 | tf_op jit(solution)/shard_map/reduce_scatter | solution.py:63
  517.9 92.5 %reduce-scatter.6.cloned.1.call-done = bf16[512,512]{1,0:T(8,128)(2,1)} async-done(((bf16[512,4096]{1,0:T(8,128)(2,1)}), bf16[512,512]{1,0:T(8,128)(2,1)}) %reduce-scatter.6.cloned.1.call-update) | async-done | bytes 524304 | tf_op jit(solution)/shard_map/reduce_scatter | solution.py:47
  (46 shorter events, 18.4 us)
Async XLA Ops:
  7.2 2.9 copy-start.3
  7.2 3.5 copy-start.2
  7.2 80.6 %all-gather.11.cloned.1.call-start = ((), (), s32[]{:S(2)}) async-start(), calls=%async_computation.9 | async-start | bytes 4718592 | tf_op jit(solution)/shard_map/all_gather | solution.py:50
  7.9 126.1 %all-gather.5.cloned.1.call-start = ((), (), s32[]{:S(2)}) async-start(), calls=%async_computation.5 | async-start | bytes 7864320 | tf_op jit(solution)/shard_map/all_gather | solution.py:27
  8.7 173.3 %all-gather.7.cloned.1.call-start = ((), (), s32[]{:S(2)}) async-start(), calls=%async_computation.6 | async-start | bytes 7864320 | tf_op jit(solution)/shard_map/all_gather | solution.py:28
  9.4 220.5 %all-gather.9.cloned.1.call-start = ((), (), s32[]{:S(2)}) async-start(), calls=%async_computation.7 | async-start | bytes 7864320 | tf_op jit(solution)/shard_map/all_gather | solution.py:29
  10.0 329.5 %reduce-scatter.14.cloned.1.call-start = ((), (), s32[]{:S(2)}) async-start(), calls=%async_computation.13 | async-start | bytes 7864320 | tf_op jit(solution)/shard_map/reduce_scatter | solution.py:76
  229.9 8.9 %copy-start = (f32[384,4096]{1,0:T(8,128)S(1)}, f32[384,4096]{1,0:T(8,128)}, u32[]{:S(2)}) copy-start(f32[384,4096]{1,0:T(8,128)} %fusion.4) | copy-start | bytes 18874372
  237.9 0.8 copy-start.1
  237.9 14.6 %copy-start.4 = (bf16[384,768]{1,0:T(8,128)(2,1)}, bf16[384,768]{1,0:T(8,128)(2,1)S(1)}, u32[]{:S(2)}) copy-start(bf16[384,768]{1,0:T(8,128)(2,1)S(1)} %get-tuple-element.11) | copy-start | bytes 1769476
  244.3 119.5 %reduce-scatter.10.cloned.1.call-start = ((), (), s32[]{:S(2)}) async-start(), calls=%async_computation.11 | async-start | bytes 7864320 | tf_op jit(solution)/shard_map/reduce_scatter | solution.py:70
  252.5 172.3 %reduce-scatter.12.cloned.1.call-start = ((), (), s32[]{:S(2)}) async-start(), calls=%async_computation.12 | async-start | bytes 7864320 | tf_op jit(solution)/shard_map/reduce_scatter | solution.py:73
  261.4 256.5 %reduce-scatter.8.cloned.1.call-start = ((), (), s32[]{:S(2)}) async-start(), calls=%async_computation.10 | async-start | bytes 4718592 | tf_op jit(solution)/shard_map/reduce_scatter | solution.py:63
  261.5 5.0 copy-start.5
  297.0 313.4 %reduce-scatter.6.cloned.1.call-start = ((), (), s32[]{:S(2)}) async-start(), calls=%async_computation.8 | async-start | bytes 4718592 | tf_op jit(solution)/shard_map/reduce_scatter | solution.py:47
Sparse Core Ops, SparseCore 0:
  10.1 77.7 all-gather.10
  89.4 44.5 all-gather.4
  135.5 46.3 all-gather.6
  183.4 46.4 all-gather.8
  244.5 58.3 reduce-scatter.13
  305.4 58.3 reduce-scatter.9
  366.4 58.3 reduce-scatter.11
  429.4 88.4 reduce-scatter.7
  522.1 88.2 reduce-scatter.5
where the time goes:
time: 617 us
  waiting for transfers between devices  456 us (74%)
  matrix products  78.8 us (13%)
  other arithmetic  24.5 us (4%)
  blocking collectives  22.3 us (4%)
  local copies, waits for them, and re-layouts  20.5 us (3%)
  between operations  14 us (2%)
    reduce_scatter x1, waiting for transfers between devices, local(): lax.psum_scatter(row_terms.astype(jnp.bfloat16), 'owner', scatter_dimensi...  92.5 us
    reduce_scatter x1, waiting for transfers between devices, local(): lax.psum_scatter(input_terms.astype(jnp.bfloat16), 'owner', scatter_dimen...  89.8 us
    all_gather x1, waiting for transfers between devices, local(): d_full = lax.all_gather(d_out, 'owner', axis=1, tiled=True)  71.2 us
    reduce_scatter x1, waiting for transfers between devices, local(): lax.psum_scatter(up_term.astype(jnp.bfloat16), 'dp', scatter_dimension=0,...  57.6 us
    all_gather x1, waiting for transfers between devices, local(): lax.all_gather(w_up, 'dp', axis=0, tiled=True)  41.6 us
    all_gather x1, waiting for transfers between devices, local(): lax.all_gather(w_down, 'dp', axis=1, tiled=True)  40.6 us
    all_gather x1, waiting for transfers between devices, local(): lax.all_gather(w_gate, 'dp', axis=0, tiled=True)  39.5 us
    dot_general x3, matrix products, contract_rows(): lax.dot_general(left, right, (((0,), (0,)), ((), ())), preferred_element_...  22.4 us
  transfers between devices with their start and end apart: 9, of which 8 were waited for; matrix products, arithmetic and copies ran while one was open for 18% of the time, Pallas kernels for 0%

commit v1 on v0

--- a/solution.py
+++ b/solution.py
@@ -4,6 +4,9 @@
 from jax.sharding import PartitionSpec as P
 
 EXPERTS = 4
+XDEPTH = 1
+BF = jnp.bfloat16
+F32 = jnp.float32
 
 
 def contract_rows(left, right):
@@ -18,7 +21,11 @@
     )
 
 
-def local(tokens, route, gate_prob, w_gate, w_up, w_down, d_out):
+def dot(left, right):
+    return jnp.dot(left, right, preferred_element_type=jnp.float32)
+
+
+def gathered(tokens, route, gate_prob, w_gate, w_up, w_down, d_out):
     row_count = tokens.shape[0]
     capacity = 3 * row_count // 4
     pieces = lax.axis_size("owner") // EXPERTS
@@ -34,21 +41,21 @@
     slot_ids = jnp.arange(capacity, dtype=jnp.int32)
     one_hot = jnp.logical_and(slot_index[None, :] == slot_ids[:, None], selected[None, :])
     dispatch = one_hot.astype(jnp.bfloat16)
-    slot_tokens = jnp.dot(dispatch, tokens, preferred_element_type=jnp.float32).astype(jnp.bfloat16)
+    slot_tokens = dot(dispatch, tokens).astype(jnp.bfloat16)
     slot_probs = jnp.sum(jnp.where(one_hot, gate_prob[None, :], jnp.float32(0.0)), axis=1)
     row_weights = jnp.where(selected, gate_prob, jnp.float32(0.0))
-    gate_pre = jnp.dot(slot_tokens, full_gate, preferred_element_type=jnp.float32)
-    up_pre = jnp.dot(slot_tokens, full_up, preferred_element_type=jnp.float32)
+    gate_pre = dot(slot_tokens, full_gate)
+    up_pre = dot(slot_tokens, full_up)
     sigma = jax.nn.sigmoid(gate_pre)
     active = gate_pre * sigma
     hidden = (active * up_pre).astype(jnp.bfloat16)
-    expert_out = jnp.dot(hidden, full_down, preferred_element_type=jnp.float32)
+    expert_out = dot(hidden, full_down)
     row_terms = jnp.take(expert_out, safe_index, axis=0) * row_weights[:, None]
     mixed = lax.psum_scatter(
         row_terms.astype(jnp.bfloat16), "owner", scatter_dimension=1, tiled=True
     )
     d_full = lax.all_gather(d_out, "owner", axis=1, tiled=True)
-    slot_cotangent = jnp.dot(dispatch, d_full, preferred_element_type=jnp.float32)
+    slot_cotangent = dot(dispatch, d_full)
     slot_router = jnp.sum(slot_cotangent * expert_out, axis=1)
     router_terms = jnp.where(selected, jnp.take(slot_router, safe_index), jnp.float32(0.0))
     grad_gate = lax.psum(router_terms, "owner")
@@ -80,6 +87,228 @@
     return (mixed, grad_tokens, grad_gate, grad_w_gate, grad_w_up, grad_w_down)
 
 
+def swap(value, axis, bit):
+    pairs = [(i, i ^ bit) for i in range(lax.axis_size(axis))]
+    return lax.ppermute(value, axis, pairs)
+
+
+def after(value, *others):
+    return lax.optimization_barrier((value,) + others)[0]
+
+
+class Line:
+    def __init__(self, axis, depth):
+        self.axis, self.depth, self.done = axis, depth, []
+
+    def __call__(self, value, bit):
+        if len(self.done) >= self.depth:
+            value = after(value, self.done[-self.depth])
+        self.done.append(swap(value, self.axis, bit))
+        return self.done[-1]
+
+
+def take_cols(value, index, width):
+    return lax.dynamic_slice_in_dim(value, index * width, width, axis=1)
+
+
+def exchanged(tokens, route, gate_prob, w_gate, w_up, w_down, d_out):
+    rows, width = tokens.shape
+    capacity = 3 * rows // 4
+    quarter = width // 4
+    part = d_out.shape[1]
+    d = lax.axis_index("dp")
+    owner = lax.axis_index("owner")
+    z, x = owner // 2, owner % 2
+    y_line, x_line = Line("dp", 1), Line("owner", XDEPTH)
+
+    def by_core(value):
+        return swap(value, "dp", 1)
+
+    def by_y(value):
+        return y_line(value, 2)
+
+    def by_x(value):
+        return x_line(value, 1)
+
+    def over_z(blocks):
+        groups = [[2 * i + j for i in range(EXPERTS)] for j in range(2)]
+        got = lax.all_to_all(blocks, "owner", 0, 0, tiled=True, axis_index_groups=groups)
+        return got.reshape(EXPERTS, -1, part)
+
+    experts = jnp.arange(EXPERTS, dtype=jnp.int32)[:, None]
+    member = route.T == experts
+    rank = jnp.cumsum(member.astype(jnp.int32), axis=1) - 1
+    rank = jnp.sum(jnp.where(member, rank, 0), axis=0)
+    own_slot = jnp.where(route[:, 0] == z, rank, -1)
+    own_place = (own_slot[None, :] == jnp.arange(capacity, dtype=jnp.int32)[:, None]).astype(BF)
+    slot = rank + route[:, 0] * capacity
+    hot = slot[None, :] == jnp.arange(EXPERTS * capacity, dtype=jnp.int32)[:, None]
+    place = hot.astype(BF)
+
+    def x_cols(k):
+        return take_cols(tokens, d ^ k, quarter)
+
+    x_got = by_y(dot(own_place, x_cols(2 + x)).astype(BF))
+    x_own = [dot(own_place, x_cols(k)).astype(BF) for k in (0, 1)]
+
+    d_expert = (gate_prob[:, None] * d_out.astype(F32)).astype(BF)
+    cot_got = over_z(dot(place, d_expert).astype(BF))
+
+    core_gate, core_up, core_down = by_core(w_gate), by_core(w_up), by_core(w_down)
+
+    def projected(x_rows):
+        return (
+            dot(x_rows[0], w_gate) + dot(x_rows[1], core_gate),
+            dot(x_rows[0], w_up) + dot(x_rows[1], core_up),
+        )
+
+    def joined(pair):
+        return jnp.concatenate([v.astype(BF) for v in pair], axis=1)
+
+    part_own = projected(x_own)
+    sent_own = joined(part_own)
+    far_rem = by_y(sent_own)
+    x_other = by_x(x_got)
+    x_rem = [jnp.where(x == 0, x_got, x_other), jnp.where(x == 0, x_other, x_got)]
+    part_rem = projected(x_rem)
+    sent_rem = joined(part_rem)
+    far_own = by_y(sent_rem)
+
+    def down_of(j):
+        return jnp.concatenate([take_cols(own_down, j, part), take_cols(core_down, j, part)], axis=1)
+
+    def rows_of(own, core, j):
+        def cut(value):
+            return lax.dynamic_slice_in_dim(value, j * part, part, axis=0)
+
+        return jnp.concatenate([cut(own), cut(core)], axis=0)
+
+    own_gate, own_up, own_down, core_gate, core_up, core_down, _ = lax.optimization_barrier(
+        (w_gate, w_up, w_down, core_gate, core_up, core_down, sent_own)
+    )
+    down_mine, down_other = down_of(x), down_of(1 - x)
+    gate_mine, gate_other = (rows_of(own_gate, core_gate, j) for j in (x, 1 - x))
+    up_mine, up_other = (rows_of(own_up, core_up, j) for j in (x, 1 - x))
+
+    def cot_at(k):
+        return lax.dynamic_index_in_dim(cot_got, d ^ k, axis=0, keepdims=False)
+
+    cot_rem = by_y(jnp.concatenate([cot_at(2), cot_at(3)], axis=1))
+    cot_own = jnp.concatenate([cot_at(0), cot_at(1)], axis=1)
+    cot_own_other = by_x(cot_own)
+
+    def back_of(mine, other):
+        return contract_cols(mine, down_mine) + contract_cols(other, down_other)
+
+    def forward(pair, far):
+        n = pair[0].shape[1]
+        gate_pre = pair[0] + far[:, :n].astype(F32)
+        up_pre = pair[1] + far[:, n:].astype(F32)
+        sigma = jax.nn.sigmoid(gate_pre)
+        active = gate_pre * sigma
+        return gate_pre, up_pre, sigma, active, (active * up_pre).astype(BF)
+
+    def backward(pre, back, far):
+        gate_pre, up_pre, sigma, active, hidden = pre
+        d_hidden = back + far.astype(F32)
+        d_gate = (d_hidden * up_pre * sigma * (1.0 + gate_pre * (1.0 - sigma))).astype(BF)
+        d_up = (d_hidden * active).astype(BF)
+        return d_gate, d_up, jnp.sum(hidden.astype(F32) * d_hidden, axis=1)
+
+    pre_own, pre_rem = forward(part_own, far_own), forward(part_rem, far_rem)
+    hidden_own, hidden_rem = pre_own[-1], pre_rem[-1]
+
+    def added(mine, got):
+        return (mine + got.astype(F32)).astype(BF)
+
+    def output(hidden):
+        return dot(hidden, down_mine), dot(hidden, down_other)
+
+    def d_input(d_gate, d_up):
+        return (
+            contract_cols(d_gate, gate_mine) + contract_cols(d_up, up_mine),
+            contract_cols(d_gate, gate_other) + contract_cols(d_up, up_other),
+        )
+
+    def plane_blocks(near, far, note=None):
+        blocks = jnp.stack([near[:, :part], near[:, part:], far[:, :part], far[:, part:]])
+        sent = [lax.dynamic_index_in_dim(blocks, d ^ i, axis=0, keepdims=False) for i in range(EXPERTS)]
+        if note is not None:
+            sent = [v for value in sent for v in (value, note)]
+        return jnp.concatenate(sent, axis=0)
+
+    def placed(got):
+        return contract_rows(place, got[:, :capacity].reshape(EXPERTS * capacity, part))
+
+    def noted(value):
+        first = value.astype(BF)
+        second = (value - first.astype(F32)).astype(BF)
+        third = (value - first.astype(F32) - second.astype(F32)).astype(BF)
+        lines = jnp.stack([first, second, third])
+        return jnp.pad(lines, ((0, 13), (0, part - value.shape[0])))
+
+    def read_note(lines):
+        return jnp.sum(lines[:3, :capacity].astype(F32), axis=0)
+
+    back_own = back_of(cot_own, cot_own_other)
+    back_far_rem = by_y(back_own.astype(BF))
+
+    mine, other = output(hidden_rem)
+    out_got = by_x(other.astype(BF))
+    cot_rem_other = by_x(cot_rem)
+    out_rem = added(mine, out_got)
+    out_far = by_y(out_rem)
+    out_mine, out_other = output(hidden_own)
+    out_near = added(out_mine, by_x(out_other.astype(BF)))
+
+    back_rem = back_of(cot_rem, cot_rem_other)
+    back_far_own = by_y(after(back_rem.astype(BF), out_near))
+    out_sent = plane_blocks(out_near, out_far)
+    out_blocks = over_z(out_sent)
+    back_far_rem, back_far_own, _ = lax.optimization_barrier((back_far_rem, back_far_own, out_sent))
+
+    d_gate_rem, d_up_rem, _ = backward(pre_rem, back_rem, back_far_rem)
+    d_gate_own, d_up_own, router = backward(pre_own, back_own, back_far_own)
+    mine, other = d_input(d_gate_rem, d_up_rem)
+    in_far = by_y(added(mine, by_x(other.astype(BF))))
+    mine, other = d_input(d_gate_own, d_up_own)
+    wide = jnp.pad(noted(router), ((0, 0), (0, other.shape[1] - part)))
+    in_sent = jnp.concatenate([other.astype(BF), wide], axis=0)
+    in_got = by_x(in_sent)
+    in_near = added(mine, in_got[:capacity])
+    in_blocks = over_z(
+        plane_blocks(in_near, in_far, noted(router + read_note(in_got[capacity:])))
+    )
+
+    notes = jnp.concatenate([read_note(v) for v in in_blocks[:, capacity:]])
+    grad_gate = jnp.sum(jnp.where(hot, notes[:, None], F32(0.0)), axis=0) / gate_prob
+    mixed = (gate_prob[:, None] * placed(out_blocks)).astype(BF)
+    grad_tokens = placed(in_blocks).astype(BF)
+
+    d_gate_own, d_gate_rem, d_up_own, d_up_rem, _ = lax.optimization_barrier(
+        (d_gate_own, d_gate_rem, d_up_own, d_up_rem, in_sent)
+    )
+    hidden_own, hidden_rem, _ = lax.optimization_barrier((hidden_own, hidden_rem, in_sent))
+    x_keep, x_give = (jnp.concatenate([own, rem], axis=0) for own, rem in zip(x_own, x_rem))
+    mine_all = jnp.concatenate([cot_own, cot_rem], axis=0)
+    other_all = jnp.concatenate([cot_own_other, cot_rem_other], axis=0)
+    d_gate_all = jnp.concatenate([d_gate_own, d_gate_rem], axis=0)
+    d_up_all = jnp.concatenate([d_up_own, d_up_rem], axis=0)
+    hidden_all = jnp.concatenate([hidden_own, hidden_rem], axis=0)
+
+    def in_chip(keep, give):
+        return keep + by_core(give.astype(BF)).astype(F32)
+
+    grad_w_gate = in_chip(contract_rows(x_keep, d_gate_all), contract_rows(x_give, d_gate_all))
+    grad_w_up = in_chip(contract_rows(x_keep, d_up_all), contract_rows(x_give, d_up_all))
+    down_keep = jnp.concatenate([mine_all[:, :part], other_all[:, :part]], axis=1)
+    down_give = jnp.concatenate([mine_all[:, part:], other_all[:, part:]], axis=1)
+    grad_down = in_chip(contract_rows(hidden_all, down_keep), contract_rows(hidden_all, down_give))
+    turned = jnp.concatenate([grad_down[:, part:], grad_down[:, :part]], axis=1)
+    grad_w_down = jnp.where(x == 0, grad_down, turned)
+    return (mixed, grad_tokens, grad_gate, grad_w_gate, grad_w_up, grad_w_down)
+
+
 def solution(mesh):
     in_specs = (
         P("dp", None),
@@ -98,4 +327,5 @@
         P("dp", "owner"),
         P("owner", "dp"),
     )
+    local = exchanged if (mesh.shape["dp"], mesh.shape["owner"]) == (4, 8) else gathered
     return jax.shard_map(local, mesh=mesh, in_specs=in_specs, out_specs=out_specs, check_vma=False)

time: 617 us -> 238 us (0.39)
  waiting for transfers between devices: 456 us -> 100 us
  starting transfers between devices: 0.36 us -> 34.3 us
  blocking collectives: 22.3 us -> 0 us
  matrix products: 78.8 us -> 57.6 us
  between operations: 14 us -> 2.03 us
  other arithmetic: 24.5 us -> 16.4 us
    reduce_scatter x5 -> x0, waiting for transfers between devices: 261 us -> none  [the longest x1 92.5 us: local(): lax.psum_scatter(row_terms.astype(jnp.bfloat16), 'owner', scatter_dimensi...]
    all_gather x4 -> x0, waiting for transfers between devices: 193 us -> none  [the longest x1 71.2 us: local(): d_full = lax.all_gather(d_out, 'owner', axis=1, tiled=True)]
    ppermute x0 -> x21, waiting for transfers between devices: none -> 88 us  [swap(): return lax.ppermute(value, axis, pairs)]
    psum x1 -> x0, blocking collectives: 22.3 us -> none  [local(): grad_gate = lax.psum(router_terms, 'owner')]
    ppermute x0 -> x21, starting transfers between devices: none -> 20.6 us  [swap(): return lax.ppermute(value, axis, pairs)]
    gather x3 -> x0, local copies, waits for them, and re-layouts: 19.5 us -> none  [the longest x1 11.6 us: local(): row_terms = jnp.take(expert_out, safe_index, axis=0) * row_weights[:, None]]
    convert_element_type x5 -> x7, other arithmetic: 23.8 us -> 5.93 us  [the longest x1 2.75 us: backward(): (d_hidden * up_pre * sigma * (1.0 + gate_pre * (1.0 - sigma))).astype(BF)]
    dot_general x5 -> x16, matrix products: 36 us -> 21.6 us  [dot(): return jnp.dot(left, right, preferred_element_type=jnp.float32)]
  transfers between devices with their start and end apart: 9 -> 24, of which waited for: 8 -> 15; matrix products, arithmetic and copies ran while one was open for 18% -> 36% of each run, Pallas kernels for 0% -> 0%
where the time goes in v1:
time: 238 us; the launch traced here: 235 us
  waiting for transfers between devices  100 us (42%)
  matrix products  57.6 us (24%)
  starting transfers between devices  34.3 us (14%)
  local copies, waits for them, and re-layouts  23.8 us (10%)
  other arithmetic  16.4 us (7%)
    ppermute x21, waiting for transfers between devices, swap(): return lax.ppermute(value, axis, pairs)  88 us
    dot_general x8, matrix products, contract_rows(): lax.dot_general(left, right, (((0,), (0,)), ((), ())), preferred_element_...  23.7 us
    dot_general x16, matrix products, dot(): return jnp.dot(left, right, preferred_element_type=jnp.float32)  21.6 us
    ppermute x21, starting transfers between devices, swap(): return lax.ppermute(value, axis, pairs)  20.6 us
    all_to_all x3, starting transfers between devices, over_z(): lax.all_to_all(blocks, 'owner', 0, 0, tiled=True, axis_index_groups=groups)  13.7 us
    all_to_all x3, waiting for transfers between devices, over_z(): lax.all_to_all(blocks, 'owner', 0, 0, tiled=True, axis_index_groups=groups)  12.5 us
    dot_general x12, matrix products, contract_cols(): lax.dot_general(left, right, (((1,), (1,)), ((), ())), preferred_element_...  12.2 us
    unnamed x110, local copies, waits for them, and re-layouts  9.79 us
  transfers between devices with their start and end apart: 24, of which 15 were waited for; matrix products, arithmetic and copies ran while one was open for 36% of the time, Pallas kernels for 0%

profile of v1, /device:TPU:0, one launch (start us, length us, event | category | flops | bytes accessed | tf_op | source)
XLA Modules:
  0.0 234.6 jit_solution(6560692664457351825)
XLA Ops:
  7.6 3.0 %collective-permute-start.1 = (bf16[384,1024]{1,0:T(8,128)(2,1)S(1)}, bf16[384,1024]{1,0:T(8,128)(2,1)S(1)}, u32[]{:S(2)}, u32[]{:S(2)}) collective-permute-start(bf16[384,1024]{1,0:T(8,128)(2,1)S(1)} %convolution_convert_fusion.5), channel_id=1, source_target_pairs={{0,16},{8,24},{16,0},{24,8},{1,17},{9,25},{17,1},{25,9},{2,18},{10... | collective-permute-start | bytes 2359304 | tf_op jit(solution)/shard_map/ppermute | solution.py:92
  12.8 5.0 %all-to-all-start = ((bf16[4,384,512]{2,1,0:T(8,128)(2,1)}), bf16[4,384,512]{2,1,0:T(8,128)(2,1)}, u32[]{:S(2)}, u32[]{:S(2)}) async-start(bf16[4,384,512]{2,1,0:T(8,128)(2,1)} %bitcast.3), calls=%async_computation | async-start | bytes 3145728 | tf_op jit(solution)/shard_map/all_to_all | solution.py:135
  24.4 4.0 %collective-permute-done.1 = bf16[384,1024]{1,0:T(8,128)(2,1)S(1)} collective-permute-done((bf16[384,1024]{1,0:T(8,128)(2,1)S(1)}, bf16[384,1024]{1,0:T(8,128)(2,1)S(1)}, u32[]{:S(2)}, u32[]{:S(2)}) %collective-permute-start.1) | collective-permute-done | bytes 786464 | tf_op jit(solution)/shard_map/ppermute | solution.py:92
  35.1 12.4 %collective-permute-done.2 = bf16[384,1024]{1,0:T(8,128)(2,1)S(1)} collective-permute-done((bf16[384,1024]{1,0:T(8,128)(2,1)S(1)}, bf16[384,1024]{1,0:T(8,128)(2,1)S(1)}, u32[]{:S(2)}, u32[]{:S(2)}) %collective-permute-start.2) | collective-permute-done | bytes 786464 | tf_op jit(solution)/shard_map/ppermute | solution.py:92
  47.6 3.9 %constant_dynamic-slice_fusion.10 = (bf16[768,512]{1,0:T(8,128)(2,1)S(1)}, bf16[768,512]{1,0:T(8,128)(2,1)}, bf16[768,512]{1,0:T(8,128)(2,1)}, bf16[768,512]{1,0:T(8,128)(2,1)}) fusion(bf16[768,1024]{1,0:T(8,128)(2,1)} %collective-permute-done.6, s32[]{:T(128)S(6)} %select_n.104, s32[]{:T(128)S(6)} %select_n.105, bf16[768,1024]{1,0:T(8,128)(2,1)} %param.12), kind=kLoop, calls=%fused_computation.165 | loop fusion | bytes 6291464 | tf_op jit(solution)/shard_map/dynamic_slice | solution.py:111
  55.3 5.2 %collective-permute-done.4 = bf16[384,1536]{1,0:T(8,128)(2,1)S(1)} collective-permute-done((bf16[384,1536]{1,0:T(8,128)(2,1)S(1)}, bf16[384,1536]{1,0:T(8,128)(2,1)S(1)}, u32[]{:S(2)}, u32[]{:S(2)}) %collective-permute-start.4) | collective-permute-done | bytes 1179680 | tf_op jit(solution)/shard_map/ppermute | solution.py:92
  68.3 3.1 %constant_dynamic-slice_fusion.6 = (bf16[512,768]{1,0:T(8,128)(2,1)}, bf16[512,768]{1,0:T(8,128)(2,1)}, bf16[512,768]{1,0:T(8,128)(2,1)}, bf16[512,768]{1,0:T(8,128)(2,1)}) fusion(bf16[1024,768]{1,0:T(8,128)(2,1)} %collective-permute-done, s32[]{:T(128)S(6)} %select_n.104, s32[]{:T(128)S(6)} %select_n.105, bf16[1024,768]{1,0:T(8,128)(2,1)S(1)} %copy-done.19), kind=kLoop, calls=%fused_computation.161 | loop fusion | bytes 6291464 | tf_op jit(solution)/shard_map/dynamic_slice | solution.py:182
  76.6 8.1 %collective-permute-done.8 = bf16[384,1024]{1,0:T(8,128)(2,1)S(1)} collective-permute-done((bf16[384,1024]{1,0:T(8,128)(2,1)S(1)}, bf16[384,1024]{1,0:T(8,128)(2,1)S(1)}, u32[]{:S(2)}, u32[]{:S(2)}) %collective-permute-start.8) | collective-permute-done | bytes 786464 | tf_op jit(solution)/shard_map/ppermute | solution.py:92
  85.2 5.0 %collective-permute-done.5 = bf16[384,1536]{1,0:T(8,128)(2,1)} collective-permute-done((bf16[384,1536]{1,0:T(8,128)(2,1)}, bf16[384,1536]{1,0:T(8,128)(2,1)}, u32[]{:S(2)}, u32[]{:S(2)}) %collective-permute-start.5) | collective-permute-done | bytes 1179680 | tf_op jit(solution)/shard_map/ppermute | solution.py:92
  95.4 5.8 %collective-permute-done.9 = bf16[384,1024]{1,0:T(8,128)(2,1)S(1)} collective-permute-done((bf16[384,1024]{1,0:T(8,128)(2,1)S(1)}, bf16[384,1024]{1,0:T(8,128)(2,1)S(1)}, u32[]{:S(2)}, u32[]{:S(2)}) %collective-permute-start.9) | collective-permute-done | bytes 786464 | tf_op jit(solution)/shard_map/ppermute | solution.py:92
  101.3 5.7 %collective-permute-done.7 = bf16[384,1024]{1,0:T(8,128)(2,1)S(1)} collective-permute-done((bf16[384,1024]{1,0:T(8,128)(2,1)S(1)}, bf16[384,1024]{1,0:T(8,128)(2,1)S(1)}, u32[]{:S(2)}, u32[]{:S(2)}) %collective-permute-start.7) | collective-permute-done | bytes 786464 | tf_op jit(solution)/shard_map/ppermute | solution.py:92
  112.1 10.4 %collective-permute-done.12 = bf16[384,768]{1,0:T(8,128)(2,1)S(1)} collective-permute-done((bf16[384,768]{1,0:T(8,128)(2,1)S(1)}, bf16[384,768]{1,0:T(8,128)(2,1)S(1)}, u32[]{:S(2)}, u32[]{:S(2)}) %collective-permute-start.12) | collective-permute-done | bytes 589856 | tf_op jit(solution)/shard_map/ppermute | solution.py:92
  130.3 7.2 %collective-permute-done.13 = bf16[384,1024]{1,0:T(8,128)(2,1)S(1)} collective-permute-done((bf16[384,1024]{1,0:T(8,128)(2,1)S(1)}, bf16[384,1024]{1,0:T(8,128)(2,1)S(1)}, u32[]{:S(2)}, u32[]{:S(2)}) %collective-permute-start.13) | collective-permute-done | bytes 786464 | tf_op jit(solution)/shard_map/ppermute | solution.py:92
  143.7 4.9 %all-to-all-start.1 = ((bf16[4,384,512]{2,1,0:T(8,128)(2,1)}), bf16[4,384,512]{2,1,0:T(8,128)(2,1)}, u32[]{:S(2)}, u32[]{:S(2)}) async-start(bf16[4,384,512]{2,1,0:T(8,128)(2,1)} %bitcast.98), calls=%async_computation.1 | async-start | bytes 3145728 | tf_op jit(solution)/shard_map/all_to_all | solution.py:135
  150.7 2.7 %multiply_convert_fusion.3 = (bf16[384,768]{1,0:T(8,128)(2,1)S(1)}, bf16[384,768]{1,0:T(8,128)(2,1)S(1)}, f32[384]{0:T(512)S(1)}) fusion(f32[384,768]{1,0:T(8,128)S(1)} %get-tuple-element.121, f32[384,768]{1,0:T(8,128)S(1)} %get-tuple-element.119, bf16[384,1536]{1,0:T(8,128)(2,1)} %collective-permute-done.5, f32[384,768]{1,0:T(8,128)} %get-tuple-element.124, ...), kind=kLoop, calls=%fused_computation.63 | loop fusion | flops 6487680 | bytes 7079424 | tf_op jit(solution)/shard_map/convert_element_type | solution.py:214
  167.0 10.7 %collective-permute-done.15 = bf16[384,1024]{1,0:T(8,128)(2,1)S(1)} collective-permute-done((bf16[384,1024]{1,0:T(8,128)(2,1)S(1)}, bf16[384,1024]{1,0:T(8,128)(2,1)S(1)}, u32[]{:S(2)}, u32[]{:S(2)}) %collective-permute-start.15) | collective-permute-done | bytes 786464 | tf_op jit(solution)/shard_map/ppermute | solution.py:92
  184.5 7.8 %collective-permute-done.17 = bf16[384,1024]{1,0:T(8,128)(2,1)S(1)} collective-permute-done((bf16[384,1024]{1,0:T(8,128)(2,1)S(1)}, bf16[384,1024]{1,0:T(8,128)(2,1)S(1)}, u32[]{:S(2)}, u32[]{:S(2)}) %collective-permute-start.17) | collective-permute-done | bytes 786464 | tf_op jit(solution)/shard_map/ppermute | solution.py:92
  195.0 3.8 %all-to-all-start.2 = ((bf16[4,400,512]{2,1,0:T(8,128)(2,1)}), bf16[4,400,512]{2,1,0:T(8,128)(2,1)S(1)}, u32[]{:S(2)}, u32[]{:S(2)}) async-start(bf16[4,400,512]{2,1,0:T(8,128)(2,1)} %bitcast.99), calls=%async_computation.2 | async-start | bytes 3276800 | tf_op jit(solution)/shard_map/all_to_all | solution.py:135
  198.9 2.9 %convolution_convert_fusion.2 = bf16[1024,768]{1,0:T(8,128)(2,1)S(1)} fusion(bf16[768,768]{1,0:T(8,128)(2,1)} %copy-done.43, bf16[384,1024]{1,0:T(8,128)(2,1)S(1)} %copy-done.28, bf16[384,1024]{1,0:T(8,128)(2,1)S(1)} %copy-done.11), kind=kOutput, calls=%fused_computation.12 | convolution fusion | flops 1211891712 | bytes 4325376 | tf_op jit(solution)/shard_map/dot_general | solution.py:13
  201.9 2.8 %convert_add_fusion = f32[768,1024]{1,0:T(8,128)S(1)} fusion(bf16[768,1024]{1,0:T(8,128)(2,1)} %collective-permute-done.20, bf16[768,768]{1,0:T(8,128)(2,1)S(1)} %copy-done.42, bf16[768,512]{1,0:T(8,128)(2,1)S(1)} %copy-done.24, bf16[768,512]{1,0:T(8,128)(2,1)S(1)} %copy-done.23), kind=kOutput, calls=%fused_computation.1 | convolution fusion | flops 1212678144 | bytes 7471104 | tf_op jit(solution)/shard_map/dot_general | solution.py:13
  207.5 4.6 %convert_add_fusion.1 = f32[1024,768]{1,0:T(8,128)} fusion(bf16[1024,768]{1,0:T(8,128)(2,1)} %collective-permute-done.19, bf16[768,768]{1,0:T(8,128)(2,1)S(1)} %copy-done.46, bf16[384,1024]{1,0:T(8,128)(2,1)S(1)} %copy-done.9, bf16[384,1024]{1,0:T(8,128)(2,1)S(1)} %copy-done.50), kind=kOutput, calls=%fused_computation.2 | convolution fusion | flops 1212678144 | bytes 7471104 | tf_op jit(solution)/shard_map/dot_general | solution.py:13
  212.2 3.2 %convert_add_fusion.2 = f32[1024,768]{1,0:T(8,128)} fusion(bf16[1024,768]{1,0:T(8,128)(2,1)S(1)} %collective-permute-done.18, bf16[768,768]{1,0:T(8,128)(2,1)S(1)} %copy-done.44, bf16[384,1024]{1,0:T(8,128)(2,1)S(1)} %copy-done.9, bf16[384,1024]{1,0:T(8,128)(2,1)S(1)} %copy-done.50), kind=kOutput, calls=%fused_computation.3 | convolution fusion | flops 1212678144 | bytes 7471104 | tf_op jit(solution)/shard_map/dot_general | solution.py:13
  215.3 3.2 %fusion.15 = bf16[512,512]{1,0:T(8,128)(2,1)} fusion(bf16[1536,512]{1,0:T(8,128)(2,1)} %bitcast.17, s32[512]{0:T(512)S(1)} %get-tuple-element.114, f32[512]{0:T(512)S(1)} %copy-done.47), kind=kOutput, calls=%fused_computation.54 | convolution fusion | flops 806617088 | bytes 2101248 | tf_op jit(solution)/shard_map/dot_general | solution.py:13
  218.6 12.5 %all-to-all-done.2 = bf16[4,400,512]{2,1,0:T(8,128)(2,1)S(1)} async-done(((bf16[4,400,512]{2,1,0:T(8,128)(2,1)}), bf16[4,400,512]{2,1,0:T(8,128)(2,1)S(1)}, u32[]{:S(2)}, u32[]{:S(2)}) %all-to-all-start.2) | async-done | bytes 1638432 | tf_op jit(solution)/shard_map/all_to_all | solution.py:135
  (227 shorter events, 94.5 us)
Async XLA Ops:
  0.6 29.4 %collective-permute-start.3 = (bf16[1024,768]{1,0:T(8,128)(2,1)}, bf16[1024,768]{1,0:T(8,128)(2,1)S(1)}, u32[]{:S(2)}, u32[]{:S(2)}) collective-permute-start(bf16[1024,768]{1,0:T(8,128)(2,1)} %param.11), channel_id=1, source_target_pairs={{0,8},{8,0},{16,24},{24,16},{1,9},{9,1},{17,25},{25,17},{2,10},{10... | collective-permute-start | bytes 4718600 | tf_op jit(solution)/shard_map/ppermute | solution.py:92
  1.2 30.1 %collective-permute-start = (bf16[1024,768]{1,0:T(8,128)(2,1)}, bf16[1024,768]{1,0:T(8,128)(2,1)}, u32[]{:S(2)}, u32[]{:S(2)}) collective-permute-start(bf16[1024,768]{1,0:T(8,128)(2,1)} %param.10), channel_id=1, source_target_pairs={{0,8},{8,0},{16,24},{24,16},{1,9},{9,1},{17,25},{25,17},{2,10},{10... | collective-permute-start | bytes 4718600 | tf_op jit(solution)/shard_map/ppermute | solution.py:92
  7.6 20.8 %collective-permute-start.1 = (bf16[384,1024]{1,0:T(8,128)(2,1)S(1)}, bf16[384,1024]{1,0:T(8,128)(2,1)S(1)}, u32[]{:S(2)}, u32[]{:S(2)}) collective-permute-start(bf16[384,1024]{1,0:T(8,128)(2,1)S(1)} %convolution_convert_fusion.5), channel_id=1, source_target_pairs={{0,16},{8,24},{16,0},{24,8},{1,17},{9,25},{17,1},{25,9},{2,18},{10... | collective-permute-start | bytes 2359304 | tf_op jit(solution)/shard_map/ppermute | solution.py:92
  12.8 52.6 %all-to-all-start = ((bf16[4,384,512]{2,1,0:T(8,128)(2,1)}), bf16[4,384,512]{2,1,0:T(8,128)(2,1)}, u32[]{:S(2)}, u32[]{:S(2)}) async-start(bf16[4,384,512]{2,1,0:T(8,128)(2,1)} %bitcast.3), calls=%async_computation | async-start | bytes 3145728 | tf_op jit(solution)/shard_map/all_to_all | solution.py:135
  17.8 29.8 %collective-permute-start.6 = (bf16[768,1024]{1,0:T(8,128)(2,1)}, bf16[768,1024]{1,0:T(8,128)(2,1)}, u32[]{:S(2)}, u32[]{:S(2)}) collective-permute-start(bf16[768,1024]{1,0:T(8,128)(2,1)} %param.12), channel_id=1, source_target_pairs={{0,8},{8,0},{16,24},{24,16},{1,9},{9,1},{17,25},{25,17},{2,10},{10... | collective-permute-start | bytes 4718600 | tf_op jit(solution)/shard_map/ppermute | solution.py:92
  28.4 19.1 %collective-permute-start.2 = (bf16[384,1024]{1,0:T(8,128)(2,1)S(1)}, bf16[384,1024]{1,0:T(8,128)(2,1)S(1)}, u32[]{:S(2)}, u32[]{:S(2)}) collective-permute-start(bf16[384,1024]{1,0:T(8,128)(2,1)S(1)} %collective-permute-done.1), channel_id=1, source_target_pairs={{0,1},{1,0},{2,3},{3,2},{4,5},{5,4},{6,7},{7,6},{8,9},{9,8},{10,11... | collective-permute-start | bytes 2359304 | tf_op jit(solution)/shard_map/ppermute | solution.py:92
  33.5 27.0 %collective-permute-start.4 = (bf16[384,1536]{1,0:T(8,128)(2,1)S(1)}, bf16[384,1536]{1,0:T(8,128)(2,1)S(1)}, u32[]{:S(2)}, u32[]{:S(2)}) collective-permute-start(bf16[384,1536]{1,0:T(8,128)(2,1)S(1)} %pad_maximum_fusion.13), channel_id=1, source_target_pairs={{0,16},{8,24},{16,0},{24,8},{1,17},{9,25},{17,1},{25,9},{2,18},{10... | collective-permute-start | bytes 3538952 | tf_op jit(solution)/shard_map/ppermute | solution.py:92
  63.9 26.3 %collective-permute-start.5 = (bf16[384,1536]{1,0:T(8,128)(2,1)}, bf16[384,1536]{1,0:T(8,128)(2,1)}, u32[]{:S(2)}, u32[]{:S(2)}) collective-permute-start(bf16[384,1536]{1,0:T(8,128)(2,1)} %pad_maximum_fusion.12), channel_id=1, source_target_pairs={{0,16},{8,24},{16,0},{24,8},{1,17},{9,25},{17,1},{25,9},{2,18},{10... | collective-permute-start | bytes 3538952 | tf_op jit(solution)/shard_map/ppermute | solution.py:92
  67.0 17.7 %collective-permute-start.8 = (bf16[384,1024]{1,0:T(8,128)(2,1)S(1)}, bf16[384,1024]{1,0:T(8,128)(2,1)S(1)}, u32[]{:S(2)}, u32[]{:S(2)}) collective-permute-start(bf16[384,1024]{1,0:T(8,128)(2,1)S(1)} %pad_maximum_fusion.27), channel_id=1, source_target_pairs={{0,1},{1,0},{2,3},{3,2},{4,5},{5,4},{6,7},{7,6},{8,9},{9,8},{10,11... | collective-permute-start | bytes 2359304 | tf_op jit(solution)/shard_map/ppermute | solution.py:92
  84.7 16.6 %collective-permute-start.9 = (bf16[384,1024]{1,0:T(8,128)(2,1)S(1)}, bf16[384,1024]{1,0:T(8,128)(2,1)S(1)}, u32[]{:S(2)}, u32[]{:S(2)}) collective-permute-start(bf16[384,1024]{1,0:T(8,128)(2,1)S(1)} %convolution_convert_fusion.3), channel_id=1, source_target_pairs={{0,1},{1,0},{2,3},{3,2},{4,5},{5,4},{6,7},{7,6},{8,9},{9,8},{10,11... | collective-permute-start | bytes 2359304 | tf_op jit(solution)/shard_map/ppermute | solution.py:92
  90.3 16.7 %collective-permute-start.7 = (bf16[384,1024]{1,0:T(8,128)(2,1)S(1)}, bf16[384,1024]{1,0:T(8,128)(2,1)S(1)}, u32[]{:S(2)}, u32[]{:S(2)}) collective-permute-start(bf16[384,1024]{1,0:T(8,128)(2,1)S(1)} %pad_maximum_fusion.26), channel_id=1, source_target_pairs={{0,16},{8,24},{16,0},{24,8},{1,17},{9,25},{17,1},{25,9},{2,18},{10... | collective-permute-start | bytes 2359304 | tf_op jit(solution)/shard_map/ppermute | solution.py:92
  107.0 17.7 %collective-permute-start.10 = (bf16[384,1024]{1,0:T(8,128)(2,1)S(1)}, bf16[384,1024]{1,0:T(8,128)(2,1)S(1)}, u32[]{:S(2)}, u32[]{:S(2)}) collective-permute-start(bf16[384,1024]{1,0:T(8,128)(2,1)S(1)} %collective-permute-done.7), channel_id=1, source_target_pairs={{0,1},{1,0},{2,3},{3,2},{4,5},{5,4},{6,7},{7,6},{8,9},{9,8},{10,11... | collective-permute-start | bytes 2359304 | tf_op jit(solution)/shard_map/ppermute | solution.py:92
  109.0 13.6 %collective-permute-start.12 = (bf16[384,768]{1,0:T(8,128)(2,1)S(1)}, bf16[384,768]{1,0:T(8,128)(2,1)S(1)}, u32[]{:S(2)}, u32[]{:S(2)}) collective-permute-start(bf16[384,768]{1,0:T(8,128)(2,1)S(1)} %get-tuple-element.43), channel_id=1, source_target_pairs={{0,16},{8,24},{16,0},{24,8},{1,17},{9,25},{17,1},{25,9},{2,18},{10... | collective-permute-start | bytes 1769480 | tf_op jit(solution)/shard_map/ppermute | solution.py:92
  122.5 14.9 %collective-permute-start.13 = (bf16[384,1024]{1,0:T(8,128)(2,1)S(1)}, bf16[384,1024]{1,0:T(8,128)(2,1)S(1)}, u32[]{:S(2)}, u32[]{:S(2)}) collective-permute-start(bf16[384,1024]{1,0:T(8,128)(2,1)S(1)} %add_convert_fusion.4), channel_id=1, source_target_pairs={{0,16},{8,24},{16,0},{24,8},{1,17},{9,25},{17,1},{25,9},{2,18},{10... | collective-permute-start | bytes 2359304 | tf_op jit(solution)/shard_map/ppermute | solution.py:92
  124.7 15.0 %collective-permute-start.11 = (bf16[384,1024]{1,0:T(8,128)(2,1)S(1)}, bf16[384,1024]{1,0:T(8,128)(2,1)S(1)}, u32[]{:S(2)}, u32[]{:S(2)}) collective-permute-start(bf16[384,1024]{1,0:T(8,128)(2,1)S(1)} %convolution_convert_fusion.4), channel_id=1, source_target_pairs={{0,1},{1,0},{2,3},{3,2},{4,5},{5,4},{6,7},{7,6},{8,9},{9,8},{10,11... | collective-permute-start | bytes 2359304 | tf_op jit(solution)/shard_map/ppermute | solution.py:92
  140.5 10.3 %collective-permute-start.14 = (bf16[384,768]{1,0:T(8,128)(2,1)}, bf16[384,768]{1,0:T(8,128)(2,1)}, u32[]{:S(2)}, u32[]{:S(2)}) collective-permute-start(bf16[384,768]{1,0:T(8,128)(2,1)} %get-tuple-element.46), channel_id=1, source_target_pairs={{0,16},{8,24},{16,0},{24,8},{1,17},{9,25},{17,1},{25,9},{2,18},{10... | collective-permute-start | bytes 1769480 | tf_op jit(solution)/shard_map/ppermute | solution.py:92
  143.7 50.2 %all-to-all-start.1 = ((bf16[4,384,512]{2,1,0:T(8,128)(2,1)}), bf16[4,384,512]{2,1,0:T(8,128)(2,1)}, u32[]{:S(2)}, u32[]{:S(2)}) async-start(bf16[4,384,512]{2,1,0:T(8,128)(2,1)} %bitcast.98), calls=%async_computation.1 | async-start | bytes 3145728 | tf_op jit(solution)/shard_map/all_to_all | solution.py:135
  160.0 17.6 %collective-permute-start.15 = (bf16[384,1024]{1,0:T(8,128)(2,1)S(1)}, bf16[384,1024]{1,0:T(8,128)(2,1)S(1)}, u32[]{:S(2)}, u32[]{:S(2)}) collective-permute-start(bf16[384,1024]{1,0:T(8,128)(2,1)S(1)} %add_convert_fusion.2), channel_id=1, source_target_pairs={{0,1},{1,0},{2,3},{3,2},{4,5},{5,4},{6,7},{7,6},{8,9},{9,8},{10,11... | collective-permute-start | bytes 2359304 | tf_op jit(solution)/shard_map/ppermute | solution.py:92
  164.4 37.5 %collective-permute-start.20 = (bf16[768,1024]{1,0:T(8,128)(2,1)}, bf16[768,1024]{1,0:T(8,128)(2,1)}, u32[]{:S(2)}, u32[]{:S(2)}) collective-permute-start(bf16[768,1024]{1,0:T(8,128)(2,1)} %convolution_convert_fusion), channel_id=1, source_target_pairs={{0,8},{8,0},{16,24},{24,16},{1,9},{9,1},{17,25},{25,17},{2,10},{10... | collective-permute-start | bytes 4718600 | tf_op jit(solution)/shard_map/ppermute | solution.py:92
  177.7 14.7 %collective-permute-start.16 = (bf16[400,1024]{1,0:T(8,128)(2,1)S(1)}, bf16[400,1024]{1,0:T(8,128)(2,1)S(1)}, u32[]{:S(2)}, u32[]{:S(2)}) collective-permute-start(bf16[400,1024]{1,0:T(8,128)(2,1)S(1)} %fusion.27), channel_id=1, source_target_pairs={{0,1},{1,0},{2,3},{3,2},{4,5},{5,4},{6,7},{7,6},{8,9},{9,8},{10,11... | collective-permute-start | bytes 2457608 | tf_op jit(solution)/shard_map/ppermute | solution.py:92
  180.3 12.1 %collective-permute-start.17 = (bf16[384,1024]{1,0:T(8,128)(2,1)S(1)}, bf16[384,1024]{1,0:T(8,128)(2,1)S(1)}, u32[]{:S(2)}, u32[]{:S(2)}) collective-permute-start(bf16[384,1024]{1,0:T(8,128)(2,1)S(1)} %add_convert_fusion), channel_id=1, source_target_pairs={{0,16},{8,24},{16,0},{24,8},{1,17},{9,25},{17,1},{25,9},{2,18},{10... | collective-permute-start | bytes 2359304 | tf_op jit(solution)/shard_map/ppermute | solution.py:92
  183.4 24.1 %collective-permute-start.19 = (bf16[1024,768]{1,0:T(8,128)(2,1)}, bf16[1024,768]{1,0:T(8,128)(2,1)}, u32[]{:S(2)}, u32[]{:S(2)}) collective-permute-start(bf16[1024,768]{1,0:T(8,128)(2,1)} %convolution_convert_fusion.1), channel_id=1, source_target_pairs={{0,8},{8,0},{16,24},{24,16},{1,9},{9,1},{17,25},{25,17},{2,10},{10... | collective-permute-start | bytes 4718600 | tf_op jit(solution)/shard_map/ppermute | solution.py:92
  195.0 36.0 %all-to-all-start.2 = ((bf16[4,400,512]{2,1,0:T(8,128)(2,1)}), bf16[4,400,512]{2,1,0:T(8,128)(2,1)S(1)}, u32[]{:S(2)}, u32[]{:S(2)}) async-start(bf16[4,400,512]{2,1,0:T(8,128)(2,1)} %bitcast.99), calls=%async_computation.2 | async-start | bytes 3276800 | tf_op jit(solution)/shard_map/all_to_all | solution.py:135
  201.7 10.4 %collective-permute-start.18 = (bf16[1024,768]{1,0:T(8,128)(2,1)S(1)}, bf16[1024,768]{1,0:T(8,128)(2,1)S(1)}, u32[]{:S(2)}, u32[]{:S(2)}) collective-permute-start(bf16[1024,768]{1,0:T(8,128)(2,1)S(1)} %convolution_convert_fusion.2), channel_id=1, source_target_pairs={{0,8},{8,0},{16,24},{24,16},{1,9},{9,1},{17,25},{25,17},{2,10},{10... | collective-permute-start | bytes 4718600 | tf_op jit(solution)/shard_map/ppermute | solution.py:92
  (51 other events, 217.5 us)

commit v2 on v1

--- a/solution.py
+++ b/solution.py
@@ -1,10 +1,14 @@
 import jax
 import jax.numpy as jnp
 from jax import lax
+from jax.experimental import pallas as pl
+from jax.experimental.pallas import tpu as pltpu
 from jax.sharding import PartitionSpec as P
 
 EXPERTS = 4
 XDEPTH = 1
+COST = 1024
+OWN_COST = 20 * 10**9
 BF = jnp.bfloat16
 F32 = jnp.float32
 
@@ -107,6 +111,74 @@
         return self.done[-1]
 
 
+def on_core(body, outs, *args, cost=COST):
+    vmem = pl.BlockSpec(memory_space=pltpu.VMEM)
+    return pl.pallas_call(
+        body,
+        out_shape=[jax.ShapeDtypeStruct(shape, kind) for shape, kind in outs],
+        in_specs=[pl.BlockSpec(memory_space=pltpu.SMEM)] + [vmem] * (len(args) - 1),
+        out_specs=[vmem] * len(outs),
+        compiler_params=pltpu.CompilerParams(vmem_limit_bytes=32 * 1024 * 1024),
+        cost_estimate=pl.CostEstimate(flops=cost, bytes_accessed=COST, transcendentals=0),
+    )(*args)
+
+
+BLOCK = 256
+
+
+def project_kernel(x_ref, first, second, gate, core_gate, up, core_up, out, sent):
+    x = x_ref[0]
+    swap_rows = x == 1
+    left = jnp.where(swap_rows, second[...], first[...])
+    right = jnp.where(swap_rows, first[...], second[...])
+    for i, (own, core) in enumerate(((gate, core_gate), (up, core_up))):
+        size = own.shape[1]
+        for j in range(0, size, BLOCK):
+            value = dot(left, own[:, j:j + BLOCK]) + dot(right, core[:, j:j + BLOCK])
+            out[:, i * size + j:i * size + j + BLOCK] = value
+            sent[:, i * size + j:i * size + j + BLOCK] = value.astype(BF)
+
+
+def output_kernel(x_ref, hidden, down, core_down, mine, other):
+    x = x_ref[0]
+    part = down.shape[1] // 2
+    for k, weight in enumerate((down, core_down)):
+        for j in range(0, part, BLOCK):
+            def cols(half):
+                return weight[:, pl.ds(pl.multiple_of(half * part + j, BLOCK), BLOCK)]
+
+            at = slice(k * part + j, k * part + j + BLOCK)
+            mine[:, at] = dot(hidden[...], cols(x))
+            other[:, at] = dot(hidden[...], cols(1 - x)).astype(BF)
+
+
+def back_kernel(x_ref, mine, other, down, core_down, out, sent):
+    x = x_ref[0]
+    part = down.shape[1] // 2
+    for j in range(0, down.shape[0], BLOCK):
+        value = jnp.zeros((mine.shape[0], BLOCK), F32)
+        for k, weight in enumerate((down, core_down)):
+            for half, cot in ((x, mine), (1 - x, other)):
+                cols = weight[j:j + BLOCK, pl.ds(pl.multiple_of(half * part, BLOCK), part)]
+                value = value + contract_cols(cot[:, k * part:(k + 1) * part], cols)
+        out[:, j:j + BLOCK] = value
+        sent[:, j:j + BLOCK] = value.astype(BF)
+
+
+def input_kernel(x_ref, d_gate, d_up, gate, core_gate, up, core_up, mine, other):
+    x = x_ref[0]
+    part = gate.shape[0] // 2
+    for k, (gate_k, up_k) in enumerate(((gate, up), (core_gate, core_up))):
+        for j in range(0, part, BLOCK):
+            def value(half):
+                at = pl.ds(pl.multiple_of(half * part + j, BLOCK), BLOCK)
+                return contract_cols(d_gate[...], gate_k[at, :]) + contract_cols(d_up[...], up_k[at, :])
+
+            at = slice(k * part + j, k * part + j + BLOCK)
+            mine[:, at] = value(x)
+            other[:, at] = value(1 - x).astype(BF)
+
+
 def take_cols(value, index, width):
     return lax.dynamic_slice_in_dim(value, index * width, width, axis=1)
 
@@ -148,62 +220,47 @@
     def x_cols(k):
         return take_cols(tokens, d ^ k, quarter)
 
-    x_got = by_y(dot(own_place, x_cols(2 + x)).astype(BF))
+    x_sent = dot(own_place, x_cols(2 + x)).astype(BF)
+    x_got = by_y(x_sent)
     x_own = [dot(own_place, x_cols(k)).astype(BF) for k in (0, 1)]
 
     d_expert = (gate_prob[:, None] * d_out.astype(F32)).astype(BF)
-    cot_got = over_z(dot(place, d_expert).astype(BF))
+    cot_got = over_z(dot(place, after(d_expert, x_sent)).astype(BF))
 
     core_gate, core_up, core_down = by_core(w_gate), by_core(w_up), by_core(w_down)
 
-    def projected(x_rows):
-        return (
-            dot(x_rows[0], w_gate) + dot(x_rows[1], core_gate),
-            dot(x_rows[0], w_up) + dot(x_rows[1], core_up),
-        )
-
-    def joined(pair):
-        return jnp.concatenate([v.astype(BF) for v in pair], axis=1)
-
-    part_own = projected(x_own)
-    sent_own = joined(part_own)
+    x_at, zero = jnp.reshape(x, (1,)), jnp.zeros((1,), jnp.int32)
+    size = w_gate.shape[1]
+
+    def projected(turned, first, second, cost):
+        weights = (w_gate, core_gate, w_up, core_up)
+        shape = (capacity, 2 * size)
+        return on_core(project_kernel, ((shape, F32), (shape, BF)), turned, first, second, *weights, cost=cost)
+
+    part_own, sent_own = projected(zero, *x_own, OWN_COST)
     far_rem = by_y(sent_own)
+    x_got = after(x_got, sent_own)
     x_other = by_x(x_got)
-    x_rem = [jnp.where(x == 0, x_got, x_other), jnp.where(x == 0, x_other, x_got)]
-    part_rem = projected(x_rem)
-    sent_rem = joined(part_rem)
-    far_own = by_y(sent_rem)
-
-    def down_of(j):
-        return jnp.concatenate([take_cols(own_down, j, part), take_cols(core_down, j, part)], axis=1)
-
-    def rows_of(own, core, j):
-        def cut(value):
-            return lax.dynamic_slice_in_dim(value, j * part, part, axis=0)
-
-        return jnp.concatenate([cut(own), cut(core)], axis=0)
-
-    own_gate, own_up, own_down, core_gate, core_up, core_down, _ = lax.optimization_barrier(
-        (w_gate, w_up, w_down, core_gate, core_up, core_down, sent_own)
-    )
-    down_mine, down_other = down_of(x), down_of(1 - x)
-    gate_mine, gate_other = (rows_of(own_gate, core_gate, j) for j in (x, 1 - x))
-    up_mine, up_other = (rows_of(own_up, core_up, j) for j in (x, 1 - x))
-
     def cot_at(k):
         return lax.dynamic_index_in_dim(cot_got, d ^ k, axis=0, keepdims=False)
 
-    cot_rem = by_y(jnp.concatenate([cot_at(2), cot_at(3)], axis=1))
+    cot_far = jnp.concatenate([cot_at(2), cot_at(3)], axis=1)
     cot_own = jnp.concatenate([cot_at(0), cot_at(1)], axis=1)
+    cot_rem = by_y(cot_far)
     cot_own_other = by_x(cot_own)
 
+    x_got, x_other, _, _ = lax.optimization_barrier((x_got, x_other, cot_far, cot_own))
+    x_rem = [jnp.where(x == 0, x_got, x_other), jnp.where(x == 0, x_other, x_got)]
+    part_rem, sent_rem = projected(x_at, x_got, x_other, COST)
+    far_own = by_y(sent_rem)
+
     def back_of(mine, other):
-        return contract_cols(mine, down_mine) + contract_cols(other, down_other)
+        shape = (capacity, size)
+        return on_core(back_kernel, ((shape, F32), (shape, BF)), x_at, mine, other, w_down, core_down)
 
     def forward(pair, far):
-        n = pair[0].shape[1]
-        gate_pre = pair[0] + far[:, :n].astype(F32)
-        up_pre = pair[1] + far[:, n:].astype(F32)
+        pre = pair + far.astype(F32)
+        gate_pre, up_pre = pre[:, :size], pre[:, size:]
         sigma = jax.nn.sigmoid(gate_pre)
         active = gate_pre * sigma
         return gate_pre, up_pre, sigma, active, (active * up_pre).astype(BF)
@@ -222,13 +279,13 @@
         return (mine + got.astype(F32)).astype(BF)
 
     def output(hidden):
-        return dot(hidden, down_mine), dot(hidden, down_other)
+        shape = (capacity, 2 * part)
+        return on_core(output_kernel, ((shape, F32), (shape, BF)), x_at, hidden, w_down, core_down)
 
     def d_input(d_gate, d_up):
-        return (
-            contract_cols(d_gate, gate_mine) + contract_cols(d_up, up_mine),
-            contract_cols(d_gate, gate_other) + contract_cols(d_up, up_other),
-        )
+        weights = (w_gate, core_gate, w_up, core_up)
+        shape = (capacity, 2 * part)
+        return on_core(input_kernel, ((shape, F32), (shape, BF)), x_at, d_gate, d_up, *weights)
 
     def plane_blocks(near, far, note=None):
         blocks = jnp.stack([near[:, :part], near[:, part:], far[:, :part], far[:, part:]])
@@ -250,30 +307,27 @@
     def read_note(lines):
         return jnp.sum(lines[:3, :capacity].astype(F32), axis=0)
 
-    back_own = back_of(cot_own, cot_own_other)
-    back_far_rem = by_y(back_own.astype(BF))
-
     mine, other = output(hidden_rem)
-    out_got = by_x(other.astype(BF))
+    out_rem = added(mine, by_x(other))
+    back_own, back_sent = back_of(cot_own, cot_own_other)
+    back_far_rem = by_y(back_sent)
+    out_far = by_y(out_rem)
     cot_rem_other = by_x(cot_rem)
-    out_rem = added(mine, out_got)
-    out_far = by_y(out_rem)
     out_mine, out_other = output(hidden_own)
-    out_near = added(out_mine, by_x(out_other.astype(BF)))
-
-    back_rem = back_of(cot_rem, cot_rem_other)
-    back_far_own = by_y(after(back_rem.astype(BF), out_near))
+    out_near = added(out_mine, by_x(out_other))
+    back_rem, back_sent = back_of(cot_rem, cot_rem_other)
     out_sent = plane_blocks(out_near, out_far)
     out_blocks = over_z(out_sent)
-    back_far_rem, back_far_own, _ = lax.optimization_barrier((back_far_rem, back_far_own, out_sent))
+    back_far_own = by_y(after(back_sent, out_near))
+    back_far_own = after(back_far_own, out_sent)
 
     d_gate_rem, d_up_rem, _ = backward(pre_rem, back_rem, back_far_rem)
     d_gate_own, d_up_own, router = backward(pre_own, back_own, back_far_own)
     mine, other = d_input(d_gate_rem, d_up_rem)
-    in_far = by_y(added(mine, by_x(other.astype(BF))))
+    in_far = by_y(added(mine, by_x(other)))
     mine, other = d_input(d_gate_own, d_up_own)
     wide = jnp.pad(noted(router), ((0, 0), (0, other.shape[1] - part)))
-    in_sent = jnp.concatenate([other.astype(BF), wide], axis=0)
+    in_sent = jnp.concatenate([other, wide], axis=0)
     in_got = by_x(in_sent)
     in_near = added(mine, in_got[:capacity])
     in_blocks = over_z(

time: 238 us -> 225 us (0.945)
  matrix products: 57.6 us -> 32.6 us
  Pallas kernels: 0 us -> 21.6 us
  waiting for transfers between devices: 100 us -> 89.6 us
  other arithmetic: 16.4 us -> 24.5 us
  local copies, waits for them, and re-layouts: 23.8 us -> 19.2 us
    ppermute x21, waiting for transfers between devices: 88 us -> 45.8 us  [swap(): return lax.ppermute(value, axis, pairs)]
    all_to_all x3, waiting for transfers between devices: 12.5 us -> 43.9 us  [over_z(): lax.all_to_all(blocks, 'owner', 0, 0, tiled=True, axis_index_groups=groups)]
    pallas_call x0 -> x8, Pallas kernels: none -> 21.6 us  [on_core(): pl.pallas_call(body, out_shape=[jax.ShapeDtypeStruct(shape, kind) for sha...]
    dot_general x16 -> x4, matrix products: 21.6 us -> 8.89 us  [dot(): return jnp.dot(left, right, preferred_element_type=jnp.float32)]
    dot_general x12 -> x0, matrix products: 12.2 us -> none  [contract_cols(): lax.dot_general(left, right, (((1,), (1,)), ((), ())), preferred_element_...]
    dynamic_slice x3 -> x0, local copies, waits for them, and re-layouts: 8.77 us -> none  [the longest x2 4.85 us: cut(): return lax.dynamic_slice_in_dim(value, j * part, part, axis=0)]
    unnamed x110 -> x104, local copies, waits for them, and re-layouts: 9.79 us -> 13.1 us
    convert_element_type x1 -> x2, other arithmetic: 0.76 us -> 3.39 us  [backward(): d_up = (d_hidden * active).astype(BF)]
  transfers between devices with their start and end apart: 24 -> 24, of which waited for: 15 -> 13; matrix products, arithmetic and copies ran while one was open for 36% -> 27% of each run, Pallas kernels for 0% -> 10%
where the time goes in v2:
time: 225 us; the launch traced here: 224 us
  waiting for transfers between devices  89.6 us (40%)
  starting transfers between devices  34.5 us (15%)
  matrix products  32.6 us (14%)
  other arithmetic  24.5 us (11%)
  Pallas kernels  21.6 us (10%)
  local copies, waits for them, and re-layouts  19.2 us (9%)
    ppermute x21, waiting for transfers between devices, swap(): return lax.ppermute(value, axis, pairs)  45.8 us
    all_to_all x3, waiting for transfers between devices, over_z(): lax.all_to_all(blocks, 'owner', 0, 0, tiled=True, axis_index_groups=groups)  43.9 us
    dot_general x8, matrix products, contract_rows(): lax.dot_general(left, right, (((0,), (0,)), ((), ())), preferred_element_...  23.7 us
    pallas_call x8, Pallas kernels, on_core(): pl.pallas_call(body, out_shape=[jax.ShapeDtypeStruct(shape, kind) for sha...  21.6 us
    ppermute x21, starting transfers between devices, swap(): return lax.ppermute(value, axis, pairs)  21.5 us
    all_to_all x3, starting transfers between devices, over_z(): lax.all_to_all(blocks, 'owner', 0, 0, tiled=True, axis_index_groups=groups)  13.1 us
    unnamed x104, local copies, waits for them, and re-layouts  13.1 us
    dot_general x4, matrix products, dot(): return jnp.dot(left, right, preferred_element_type=jnp.float32)  8.89 us
  transfers between devices with their start and end apart: 24, of which 13 were waited for; matrix products, arithmetic and copies ran while one was open for 27% of the time, Pallas kernels for 10%

profile of v2, /device:TPU:0, one launch (start us, length us, event | category | flops | bytes accessed | tf_op | source)
XLA Modules:
  0.0 223.6 jit_solution(1469429479133054939)
XLA Ops:
  5.8 2.7 %convolution_convert_fusion.3 = bf16[384,1024]{1,0:T(8,128)(2,1)} fusion(bf16[512,4096]{1,0:T(8,128)(2,1)} %param.7, s32[]{:T(128)S(6)} %select_n.84, s32[512]{0:T(512)S(1)} %get-tuple-element.126), kind=kOutput, calls=%fused_computation.36 | convolution fusion | flops 403243008 | bytes 1837060 | tf_op jit(solution)/shard_map/dot_general | solution.py:29
  8.5 2.9 %collective-permute-start.2 = (bf16[384,1024]{1,0:T(8,128)(2,1)}, bf16[384,1024]{1,0:T(8,128)(2,1)}, u32[]{:S(2)}, u32[]{:S(2)}) collective-permute-start(bf16[384,1024]{1,0:T(8,128)(2,1)} %convolution_convert_fusion.3), channel_id=1, source_target_pairs={{0,16},{8,24},{16,0},{24,8},{1,17},{9,25},{17,1},{25,9},{2,18},{10... | collective-permute-start | bytes 2359304 | tf_op jit(solution)/shard_map/ppermute | solution.py:96
  13.7 4.9 %all-to-all-start = ((bf16[4,384,512]{2,1,0:T(8,128)(2,1)}), bf16[4,384,512]{2,1,0:T(8,128)(2,1)}, u32[]{:S(2)}, u32[]{:S(2)}) async-start(bf16[4,384,512]{2,1,0:T(8,128)(2,1)} %bitcast.71), calls=%async_computation | async-start | bytes 3145728 | tf_op jit(solution)/shard_map/all_to_all | solution.py:207
  22.8 3.6 %shard_map.118 = (f32[384,1536]{1,0:T(8,128)S(1)}, bf16[384,1536]{1,0:T(8,128)(2,1)}) custom-call(s32[1]{0:T(128)} %constant.75.clone.1.x_ref, bf16[384,1024]{1,0:T(8,128)(2,1)S(1)} %convolution_convert_fusion.5.first, bf16[384,1024]{1,0:T(8,128)(2,1)S(1)} %convolution_convert_fusion.4.second, bf16[1024,768]{1,0:T(8,128)(2,1)S(1)} %copy-done.1, ...), custom_call_target="tpu_custom_call" | custom-call | flops 20000000000 | bytes 1024 | tf_op jit(solution)/shard_map/pallas_call | solution.py:116
  32.7 22.9 %all-to-all-done = bf16[4,384,512]{2,1,0:T(8,128)(2,1)} async-done(((bf16[4,384,512]{2,1,0:T(8,128)(2,1)}), bf16[4,384,512]{2,1,0:T(8,128)(2,1)}, u32[]{:S(2)}, u32[]{:S(2)}) %all-to-all-start) | async-done | bytes 1572896 | tf_op jit(solution)/shard_map/all_to_all | solution.py:207
  66.6 4.0 %shard_map.119 = (f32[384,1536]{1,0:T(8,128)S(1)}, bf16[384,1536]{1,0:T(8,128)(2,1)S(1)}) custom-call(s32[1]{0:T(128)} %bitcast.3.x_ref, bf16[384,1024]{1,0:T(8,128)(2,1)} %collective-permute-done.2.first, bf16[384,1024]{1,0:T(8,128)(2,1)} %collective-permute-done.3.second, bf16[1024,768]{1,0:T(8,128)(2,1)S(1)} %copy-done.2, ...), custom_call_target="tpu_custom_call" | custom-call | flops 1024 | bytes 1024 | tf_op jit(solution)/shard_map/pallas_call | solution.py:116
  70.6 7.2 %collective-permute-done.5.mine = bf16[384,1024]{1,0:T(8,128)(2,1)} collective-permute-done((bf16[384,1024]{1,0:T(8,128)(2,1)}, bf16[384,1024]{1,0:T(8,128)(2,1)}, u32[]{:S(2)}, u32[]{:S(2)}) %collective-permute-start.5) | collective-permute-done | bytes 786464 | tf_op jit(solution)/shard_map/ppermute | solution.py:96
  91.1 8.8 %collective-permute-done.9 = bf16[384,1024]{1,0:T(8,128)(2,1)S(1)} collective-permute-done((bf16[384,1024]{1,0:T(8,128)(2,1)S(1)}, bf16[384,1024]{1,0:T(8,128)(2,1)S(1)}, u32[]{:S(2)}, u32[]{:S(2)}) %collective-permute-start.9) | collective-permute-done | bytes 786464 | tf_op jit(solution)/shard_map/ppermute | solution.py:96
  107.8 10.1 %collective-permute-done.10.other = bf16[384,1024]{1,0:T(8,128)(2,1)S(1)} collective-permute-done((bf16[384,1024]{1,0:T(8,128)(2,1)}, bf16[384,1024]{1,0:T(8,128)(2,1)S(1)}, u32[]{:S(2)}, u32[]{:S(2)}) %collective-permute-start.10) | collective-permute-done | bytes 786464 | tf_op jit(solution)/shard_map/ppermute | solution.py:96
  119.4 3.6 %shard_map.123 = (f32[384,768]{1,0:T(8,128)S(1)}, bf16[384,768]{1,0:T(8,128)(2,1)}) custom-call(s32[1]{0:T(128)} %bitcast.3.x_ref, bf16[384,1024]{1,0:T(8,128)(2,1)} %collective-permute-done.5.mine, bf16[384,1024]{1,0:T(8,128)(2,1)S(1)} %collective-permute-done.10.other, bf16[768,1024]{1,0:T(8,128)(2,1)S(1)} %copy-done, ...), custom_call_target="tpu_custom_call" | custom-call | flops 1024 | bytes 1024 | tf_op jit(solution)/shard_map/pallas_call | solution.py:116
  128.6 3.5 %shard_map.125 = (f32[384,1024]{1,0:T(8,128)S(1)}, bf16[384,1024]{1,0:T(8,128)(2,1)}) custom-call(s32[1]{0:T(128)} %bitcast.3.x_ref, bf16[384,768]{1,0:T(8,128)(2,1)S(1)} %get-tuple-element.83.d_gate, bf16[384,768]{1,0:T(8,128)(2,1)S(1)} %get-tuple-element.85.d_up, bf16[1024,768]{1,0:T(8,128)(2,1)S(1)} %copy-done.2, bf16[1024,768]{1,0:T(8,128)(2,1)S(1)} %copy-done.9, ...), custom_call_target="tpu_custom_call" | custom-call | flops 1024 | bytes 1024 | tf_op jit(solution)/shard_map/pallas_call | solution.py:116
  132.1 3.3 %collective-permute-done.11 = bf16[384,1024]{1,0:T(8,128)(2,1)S(1)} collective-permute-done((bf16[384,1024]{1,0:T(8,128)(2,1)S(1)}, bf16[384,1024]{1,0:T(8,128)(2,1)S(1)}, u32[]{:S(2)}, u32[]{:S(2)}) %collective-permute-start.11) | collective-permute-done | bytes 786464 | tf_op jit(solution)/shard_map/ppermute | solution.py:96
  137.2 4.7 %collective-permute-done.13 = bf16[384,1024]{1,0:T(8,128)(2,1)S(1)} collective-permute-done((bf16[384,1024]{1,0:T(8,128)(2,1)S(1)}, bf16[384,1024]{1,0:T(8,128)(2,1)S(1)}, u32[]{:S(2)}, u32[]{:S(2)}) %collective-permute-start.13) | collective-permute-done | bytes 786464 | tf_op jit(solution)/shard_map/ppermute | solution.py:96
  144.9 4.4 %all-to-all-start.1 = ((bf16[4,384,512]{2,1,0:T(8,128)(2,1)}), bf16[4,384,512]{2,1,0:T(8,128)(2,1)}, u32[]{:S(2)}, u32[]{:S(2)}) async-start(bf16[4,384,512]{2,1,0:T(8,128)(2,1)} %bitcast.69), calls=%async_computation.1 | async-start | bytes 3145728 | tf_op jit(solution)/shard_map/all_to_all | solution.py:207
  153.4 2.8 %multiply_convert_fusion.2 = (bf16[384,768]{1,0:T(8,128)(2,1)S(1)}, bf16[384,768]{1,0:T(8,128)(2,1)S(1)}, f32[384]{0:T(512)S(1)}) fusion(f32[384,768]{1,0:T(8,128)S(1)} %copy-done.26, bf16[384,768]{1,0:T(8,128)(2,1)} %collective-permute-done.14, f32[384,1536]{1,0:T(8,128)} %copy-done.31), kind=kLoop, calls=%fused_computation.46 | loop fusion | flops 5897856 | bytes 5309952 | tf_op jit(solution)/shard_map/convert_element_type | solution.py:272
  169.7 4.1 %collective-permute-done.17 = bf16[384,1024]{1,0:T(8,128)(2,1)S(1)} collective-permute-done((bf16[384,1024]{1,0:T(8,128)(2,1)S(1)}, bf16[384,1024]{1,0:T(8,128)(2,1)S(1)}, u32[]{:S(2)}, u32[]{:S(2)}) %collective-permute-start.17) | collective-permute-done | bytes 786464 | tf_op jit(solution)/shard_map/ppermute | solution.py:96
  176.1 4.8 %all-to-all-done.1 = bf16[4,384,512]{2,1,0:T(8,128)(2,1)} async-done(((bf16[4,384,512]{2,1,0:T(8,128)(2,1)}), bf16[4,384,512]{2,1,0:T(8,128)(2,1)}, u32[]{:S(2)}, u32[]{:S(2)}) %all-to-all-start.1) | async-done | bytes 1572896 | tf_op jit(solution)/shard_map/all_to_all | solution.py:207
  180.8 3.8 %all-to-all-start.2 = ((bf16[4,400,512]{2,1,0:T(8,128)(2,1)}), bf16[4,400,512]{2,1,0:T(8,128)(2,1)S(1)}, u32[]{:S(2)}, u32[]{:S(2)}) async-start(bf16[4,400,512]{2,1,0:T(8,128)(2,1)} %bitcast.70), calls=%async_computation.2 | async-start | bytes 3276800 | tf_op jit(solution)/shard_map/all_to_all | solution.py:207
  184.7 2.9 %convolution_convert_fusion.1 = bf16[1024,768]{1,0:T(8,128)(2,1)S(1)} fusion(bf16[768,768]{1,0:T(8,128)(2,1)} %copy-done.45, bf16[384,1024]{1,0:T(8,128)(2,1)S(1)} %copy-done.39, bf16[384,1024]{1,0:T(8,128)(2,1)S(1)} %copy-done.30), kind=kOutput, calls=%fused_computation.13 | convolution fusion | flops 1211891712 | bytes 4325376 | tf_op jit(solution)/shard_map/dot_general | solution.py:17
  187.7 2.8 %convert_add_fusion = f32[768,1024]{1,0:T(8,128)S(1)} fusion(bf16[768,1024]{1,0:T(8,128)(2,1)} %collective-permute-done.20, bf16[768,768]{1,0:T(8,128)(2,1)S(1)} %copy-done.44, bf16[768,512]{1,0:T(8,128)(2,1)S(1)} %copy-done.35, bf16[768,512]{1,0:T(8,128)(2,1)S(1)} %copy-done.34), kind=kOutput, calls=%fused_computation.1 | convolution fusion | flops 1212678144 | bytes 7471104 | tf_op jit(solution)/shard_map/dot_general | solution.py:17
  193.3 4.6 %convert_add_fusion.2 = f32[1024,768]{1,0:T(8,128)} fusion(bf16[1024,768]{1,0:T(8,128)(2,1)} %collective-permute-done.18, bf16[768,768]{1,0:T(8,128)(2,1)S(1)} %copy-done.42, bf16[384,1024]{1,0:T(8,128)(2,1)S(1)} %copy-done.38, bf16[384,1024]{1,0:T(8,128)(2,1)S(1)} %copy-done.28), kind=kOutput, calls=%fused_computation.3 | convolution fusion | flops 1212678144 | bytes 7471104 | tf_op jit(solution)/shard_map/dot_general | solution.py:17
  198.0 3.2 %convert_add_fusion.1 = f32[1024,768]{1,0:T(8,128)} fusion(bf16[1024,768]{1,0:T(8,128)(2,1)S(1)} %collective-permute-done.19, bf16[768,768]{1,0:T(8,128)(2,1)S(1)} %copy-done.46, bf16[384,1024]{1,0:T(8,128)(2,1)S(1)} %copy-done.38, bf16[384,1024]{1,0:T(8,128)(2,1)S(1)} %copy-done.28), kind=kOutput, calls=%fused_computation.2 | convolution fusion | flops 1212678144 | bytes 7471104 | tf_op jit(solution)/shard_map/dot_general | solution.py:17
  201.1 3.2 %fusion.15 = bf16[512,512]{1,0:T(8,128)(2,1)} fusion(bf16[1536,512]{1,0:T(8,128)(2,1)} %bitcast.18, s32[512]{0:T(512)S(1)} %get-tuple-element.125, f32[512]{0:T(512)S(1)} %copy-done.47), kind=kOutput, calls=%fused_computation.40 | convolution fusion | flops 806617088 | bytes 2101248 | tf_op jit(solution)/shard_map/dot_general | solution.py:17
  204.4 16.2 %all-to-all-done.2 = bf16[4,400,512]{2,1,0:T(8,128)(2,1)S(1)} async-done(((bf16[4,400,512]{2,1,0:T(8,128)(2,1)}), bf16[4,400,512]{2,1,0:T(8,128)(2,1)S(1)}, u32[]{:S(2)}, u32[]{:S(2)}) %all-to-all-start.2) | async-done | bytes 1638432 | tf_op jit(solution)/shard_map/all_to_all | solution.py:207
  (206 shorter events, 87.0 us)
Async XLA Ops:
  0.6 22.1 %collective-permute-start = (bf16[1024,768]{1,0:T(8,128)(2,1)}, bf16[1024,768]{1,0:T(8,128)(2,1)S(1)}, u32[]{:S(2)}, u32[]{:S(2)}) collective-permute-start(bf16[1024,768]{1,0:T(8,128)(2,1)} %gate.7), channel_id=1, source_target_pairs={{0,8},{8,0},{16,24},{24,16},{1,9},{9,1},{17,25},{25,17},{2,10},{10... | collective-permute-start | bytes 4718600 | tf_op jit(solution)/shard_map/ppermute | solution.py:96
  1.2 21.6 %collective-permute-start.1 = (bf16[1024,768]{1,0:T(8,128)(2,1)}, bf16[1024,768]{1,0:T(8,128)(2,1)S(1)}, u32[]{:S(2)}, u32[]{:S(2)}) collective-permute-start(bf16[1024,768]{1,0:T(8,128)(2,1)} %up.7), channel_id=1, source_target_pairs={{0,8},{8,0},{16,24},{24,16},{1,9},{9,1},{17,25},{25,17},{2,10},{10... | collective-permute-start | bytes 4718600 | tf_op jit(solution)/shard_map/ppermute | solution.py:96
  8.5 21.0 %collective-permute-start.2 = (bf16[384,1024]{1,0:T(8,128)(2,1)}, bf16[384,1024]{1,0:T(8,128)(2,1)}, u32[]{:S(2)}, u32[]{:S(2)}) collective-permute-start(bf16[384,1024]{1,0:T(8,128)(2,1)} %convolution_convert_fusion.3), channel_id=1, source_target_pairs={{0,16},{8,24},{16,0},{24,8},{1,17},{9,25},{17,1},{25,9},{2,18},{10... | collective-permute-start | bytes 2359304 | tf_op jit(solution)/shard_map/ppermute | solution.py:96
  13.7 41.9 %all-to-all-start = ((bf16[4,384,512]{2,1,0:T(8,128)(2,1)}), bf16[4,384,512]{2,1,0:T(8,128)(2,1)}, u32[]{:S(2)}, u32[]{:S(2)}) async-start(bf16[4,384,512]{2,1,0:T(8,128)(2,1)} %bitcast.71), calls=%async_computation | async-start | bytes 3145728 | tf_op jit(solution)/shard_map/all_to_all | solution.py:207
  29.5 29.4 %collective-permute-start.4 = (bf16[384,1536]{1,0:T(8,128)(2,1)}, bf16[384,1536]{1,0:T(8,128)(2,1)}, u32[]{:S(2)}, u32[]{:S(2)}) collective-permute-start(bf16[384,1536]{1,0:T(8,128)(2,1)} %get-tuple-element.54), channel_id=1, source_target_pairs={{0,16},{8,24},{16,0},{24,8},{1,17},{9,25},{17,1},{25,9},{2,18},{10... | collective-permute-start | bytes 3538952 | tf_op jit(solution)/shard_map/ppermute | solution.py:96
  31.2 29.6 %collective-permute-start.3 = (bf16[384,1024]{1,0:T(8,128)(2,1)}, bf16[384,1024]{1,0:T(8,128)(2,1)}, u32[]{:S(2)}, u32[]{:S(2)}) collective-permute-start(bf16[384,1024]{1,0:T(8,128)(2,1)} %collective-permute-done.2.first), channel_id=1, source_target_pairs={{0,1},{1,0},{2,3},{3,2},{4,5},{5,4},{6,7},{7,6},{8,9},{9,8},{10,11... | collective-permute-start | bytes 2359304 | tf_op jit(solution)/shard_map/ppermute | solution.py:96
  58.9 18.8 %collective-permute-start.5 = (bf16[384,1024]{1,0:T(8,128)(2,1)}, bf16[384,1024]{1,0:T(8,128)(2,1)}, u32[]{:S(2)}, u32[]{:S(2)}) collective-permute-start(bf16[384,1024]{1,0:T(8,128)(2,1)} %pad_maximum_fusion.14), channel_id=1, source_target_pairs={{0,16},{8,24},{16,0},{24,8},{1,17},{9,25},{17,1},{25,9},{2,18},{10... | collective-permute-start | bytes 2359304 | tf_op jit(solution)/shard_map/ppermute | solution.py:96
  59.6 20.6 %collective-permute-start.7 = (bf16[768,1024]{1,0:T(8,128)(2,1)S(1)}, bf16[768,1024]{1,0:T(8,128)(2,1)S(1)}, u32[]{:S(2)}, u32[]{:S(2)}) collective-permute-start(bf16[768,1024]{1,0:T(8,128)(2,1)S(1)} %copy-done), channel_id=1, source_target_pairs={{0,8},{8,0},{16,24},{24,16},{1,9},{9,1},{17,25},{25,17},{2,10},{10... | collective-permute-start | bytes 4718600 | tf_op jit(solution)/shard_map/ppermute | solution.py:96
  60.8 20.8 %collective-permute-start.8 = (bf16[384,1024]{1,0:T(8,128)(2,1)S(1)}, bf16[384,1024]{1,0:T(8,128)(2,1)S(1)}, u32[]{:S(2)}, u32[]{:S(2)}) collective-permute-start(bf16[384,1024]{1,0:T(8,128)(2,1)S(1)} %pad_maximum_fusion.15.mine), channel_id=1, source_target_pairs={{0,1},{1,0},{2,3},{3,2},{4,5},{5,4},{6,7},{7,6},{8,9},{9,8},{10,11... | collective-permute-start | bytes 2359304 | tf_op jit(solution)/shard_map/ppermute | solution.py:96
  77.7 26.1 %collective-permute-start.6 = (bf16[384,1536]{1,0:T(8,128)(2,1)S(1)}, bf16[384,1536]{1,0:T(8,128)(2,1)S(1)}, u32[]{:S(2)}, u32[]{:S(2)}) collective-permute-start(bf16[384,1536]{1,0:T(8,128)(2,1)S(1)} %get-tuple-element.56), channel_id=1, source_target_pairs={{0,16},{8,24},{16,0},{24,8},{1,17},{9,25},{17,1},{25,9},{2,18},{10... | collective-permute-start | bytes 3538952 | tf_op jit(solution)/shard_map/ppermute | solution.py:96
  81.6 18.4 %collective-permute-start.9 = (bf16[384,1024]{1,0:T(8,128)(2,1)S(1)}, bf16[384,1024]{1,0:T(8,128)(2,1)S(1)}, u32[]{:S(2)}, u32[]{:S(2)}) collective-permute-start(bf16[384,1024]{1,0:T(8,128)(2,1)S(1)} %get-tuple-element.62), channel_id=1, source_target_pairs={{0,1},{1,0},{2,3},{3,2},{4,5},{5,4},{6,7},{7,6},{8,9},{9,8},{10,11... | collective-permute-start | bytes 2359304 | tf_op jit(solution)/shard_map/ppermute | solution.py:96
  100.0 17.9 %collective-permute-start.10 = (bf16[384,1024]{1,0:T(8,128)(2,1)}, bf16[384,1024]{1,0:T(8,128)(2,1)S(1)}, u32[]{:S(2)}, u32[]{:S(2)}) collective-permute-start(bf16[384,1024]{1,0:T(8,128)(2,1)} %collective-permute-done.5.mine), channel_id=1, source_target_pairs={{0,1},{1,0},{2,3},{3,2},{4,5},{5,4},{6,7},{7,6},{8,9},{9,8},{10,11... | collective-permute-start | bytes 2359304 | tf_op jit(solution)/shard_map/ppermute | solution.py:96
  103.9 20.6 %collective-permute-start.12 = (bf16[384,768]{1,0:T(8,128)(2,1)S(1)}, bf16[384,768]{1,0:T(8,128)(2,1)S(1)}, u32[]{:S(2)}, u32[]{:S(2)}) collective-permute-start(bf16[384,768]{1,0:T(8,128)(2,1)S(1)} %get-tuple-element.67), channel_id=1, source_target_pairs={{0,16},{8,24},{16,0},{24,8},{1,17},{9,25},{17,1},{25,9},{2,18},{10... | collective-permute-start | bytes 1769480 | tf_op jit(solution)/shard_map/ppermute | solution.py:96
  117.9 17.5 %collective-permute-start.11 = (bf16[384,1024]{1,0:T(8,128)(2,1)S(1)}, bf16[384,1024]{1,0:T(8,128)(2,1)S(1)}, u32[]{:S(2)}, u32[]{:S(2)}) collective-permute-start(bf16[384,1024]{1,0:T(8,128)(2,1)S(1)} %get-tuple-element.64), channel_id=1, source_target_pairs={{0,1},{1,0},{2,3},{3,2},{4,5},{5,4},{6,7},{7,6},{8,9},{9,8},{10,11... | collective-permute-start | bytes 2359304 | tf_op jit(solution)/shard_map/ppermute | solution.py:96
  124.4 17.5 %collective-permute-start.13 = (bf16[384,1024]{1,0:T(8,128)(2,1)S(1)}, bf16[384,1024]{1,0:T(8,128)(2,1)S(1)}, u32[]{:S(2)}, u32[]{:S(2)}) collective-permute-start(bf16[384,1024]{1,0:T(8,128)(2,1)S(1)} %add_convert_fusion.2), channel_id=1, source_target_pairs={{0,16},{8,24},{16,0},{24,8},{1,17},{9,25},{17,1},{25,9},{2,18},{10... | collective-permute-start | bytes 2359304 | tf_op jit(solution)/shard_map/ppermute | solution.py:96
  135.4 16.0 %collective-permute-start.15 = (bf16[384,1024]{1,0:T(8,128)(2,1)}, bf16[384,1024]{1,0:T(8,128)(2,1)}, u32[]{:S(2)}, u32[]{:S(2)}) collective-permute-start(bf16[384,1024]{1,0:T(8,128)(2,1)} %get-tuple-element.78), channel_id=1, source_target_pairs={{0,1},{1,0},{2,3},{3,2},{4,5},{5,4},{6,7},{7,6},{8,9},{9,8},{10,11... | collective-permute-start | bytes 2359304 | tf_op jit(solution)/shard_map/ppermute | solution.py:96
  141.9 11.4 %collective-permute-start.14 = (bf16[384,768]{1,0:T(8,128)(2,1)}, bf16[384,768]{1,0:T(8,128)(2,1)}, u32[]{:S(2)}, u32[]{:S(2)}) collective-permute-start(bf16[384,768]{1,0:T(8,128)(2,1)} %get-tuple-element.72), channel_id=1, source_target_pairs={{0,16},{8,24},{16,0},{24,8},{1,17},{9,25},{17,1},{25,9},{2,18},{10... | collective-permute-start | bytes 1769480 | tf_op jit(solution)/shard_map/ppermute | solution.py:96
  144.9 35.9 %all-to-all-start.1 = ((bf16[4,384,512]{2,1,0:T(8,128)(2,1)}), bf16[4,384,512]{2,1,0:T(8,128)(2,1)}, u32[]{:S(2)}, u32[]{:S(2)}) async-start(bf16[4,384,512]{2,1,0:T(8,128)(2,1)} %bitcast.69), calls=%async_computation.1 | async-start | bytes 3145728 | tf_op jit(solution)/shard_map/all_to_all | solution.py:207
  159.0 14.8 %collective-permute-start.17 = (bf16[384,1024]{1,0:T(8,128)(2,1)S(1)}, bf16[384,1024]{1,0:T(8,128)(2,1)S(1)}, u32[]{:S(2)}, u32[]{:S(2)}) collective-permute-start(bf16[384,1024]{1,0:T(8,128)(2,1)S(1)} %add_convert_fusion), channel_id=1, source_target_pairs={{0,16},{8,24},{16,0},{24,8},{1,17},{9,25},{17,1},{25,9},{2,18},{10... | collective-permute-start | bytes 2359304 | tf_op jit(solution)/shard_map/ppermute | solution.py:96
  160.2 15.0 %collective-permute-start.16 = (bf16[400,1024]{1,0:T(8,128)(2,1)S(1)}, bf16[400,1024]{1,0:T(8,128)(2,1)S(1)}, u32[]{:S(2)}, u32[]{:S(2)}) collective-permute-start(bf16[400,1024]{1,0:T(8,128)(2,1)S(1)} %fusion.24), channel_id=1, source_target_pairs={{0,1},{1,0},{2,3},{3,2},{4,5},{5,4},{6,7},{7,6},{8,9},{9,8},{10,11... | collective-permute-start | bytes 2457608 | tf_op jit(solution)/shard_map/ppermute | solution.py:96
  164.5 28.9 %collective-permute-start.18 = (bf16[1024,768]{1,0:T(8,128)(2,1)}, bf16[1024,768]{1,0:T(8,128)(2,1)}, u32[]{:S(2)}, u32[]{:S(2)}) collective-permute-start(bf16[1024,768]{1,0:T(8,128)(2,1)} %convolution_convert_fusion.2), channel_id=1, source_target_pairs={{0,8},{8,0},{16,24},{24,16},{1,9},{9,1},{17,25},{25,17},{2,10},{10... | collective-permute-start | bytes 4718600 | tf_op jit(solution)/shard_map/ppermute | solution.py:96
  168.6 19.1 %collective-permute-start.20 = (bf16[768,1024]{1,0:T(8,128)(2,1)}, bf16[768,1024]{1,0:T(8,128)(2,1)}, u32[]{:S(2)}, u32[]{:S(2)}) collective-permute-start(bf16[768,1024]{1,0:T(8,128)(2,1)} %convolution_convert_fusion), channel_id=1, source_target_pairs={{0,8},{8,0},{16,24},{24,16},{1,9},{9,1},{17,25},{25,17},{2,10},{10... | collective-permute-start | bytes 4718600 | tf_op jit(solution)/shard_map/ppermute | solution.py:96
  180.8 39.7 %all-to-all-start.2 = ((bf16[4,400,512]{2,1,0:T(8,128)(2,1)}), bf16[4,400,512]{2,1,0:T(8,128)(2,1)S(1)}, u32[]{:S(2)}, u32[]{:S(2)}) async-start(bf16[4,400,512]{2,1,0:T(8,128)(2,1)} %bitcast.70), calls=%async_computation.2 | async-start | bytes 3276800 | tf_op jit(solution)/shard_map/all_to_all | solution.py:207
  187.6 10.4 %collective-permute-start.19 = (bf16[1024,768]{1,0:T(8,128)(2,1)S(1)}, bf16[1024,768]{1,0:T(8,128)(2,1)S(1)}, u32[]{:S(2)}, u32[]{:S(2)}) collective-permute-start(bf16[1024,768]{1,0:T(8,128)(2,1)S(1)} %convolution_convert_fusion.1), channel_id=1, source_target_pairs={{0,8},{8,0},{16,24},{24,16},{1,9},{9,1},{17,25},{25,17},{2,10},{10... | collective-permute-start | bytes 4718600 | tf_op jit(solution)/shard_map/ppermute | solution.py:96
  (48 other events, 157.0 us)

commit v3 on v2

--- a/solution.py
+++ b/solution.py
@@ -9,6 +9,7 @@
 XDEPTH = 1
 COST = 1024
 OWN_COST = 20 * 10**9
+TERM_COST = 20 * 10**9
 BF = jnp.bfloat16
 F32 = jnp.float32
 
@@ -179,6 +180,63 @@
             other[:, at] = value(1 - x).astype(BF)
 
 
+def terms_kernel(
+    x_ref, hidden, hidden_rem, mine, mine_rem, other, other_rem,
+    tokens, got, swapped, d_gate, d_gate_rem, d_up, d_up_rem, down, gate, up
+):
+    part = mine.shape[1] // 2
+    for half, (own, rem) in enumerate(((mine, mine_rem), (other, other_rem))):
+        for j in range(0, part, BLOCK):
+            at = slice(part + j, part + j + BLOCK)
+            value = contract_rows(hidden[...], own[:, at]) + contract_rows(hidden_rem[...], rem[:, at])
+            down[:, half * part + j:half * part + j + BLOCK] = value.astype(BF)
+    tokens_rem = jnp.where(x_ref[0] == 1, got[...], swapped[...])
+    for out, own, rem in ((gate, d_gate, d_gate_rem), (up, d_up, d_up_rem)):
+        for j in range(0, out.shape[1], BLOCK):
+            at = slice(j, j + BLOCK)
+            value = contract_rows(tokens[...], own[:, at]) + contract_rows(tokens_rem, rem[:, at])
+            out[:, at] = value.astype(BF)
+
+
+def route_kernel(at_ref, route, tokens, own_place, place, sent):
+    rows, capacity = route.shape[1], own_place.shape[0]
+    chosen = route[...]
+    member = lax.broadcasted_iota(jnp.int32, (8, rows), 0) == chosen
+    member = jnp.where(member, F32(1.0), F32(0.0))
+    row, col = (lax.broadcasted_iota(jnp.int32, (rows, rows), i) for i in (0, 1))
+    upto = jnp.where(row <= col, F32(1.0), F32(0.0)).astype(BF)
+    rank = jnp.sum(member * dot(member.astype(BF), upto), axis=0, keepdims=True) - 1.0
+    slot = rank.astype(jnp.int32) + chosen * capacity
+
+    def one_hot(count, first):
+        ids = lax.broadcasted_iota(jnp.int32, (count, rows), 0) + first
+        return jnp.where(ids == slot, F32(1.0), F32(0.0)).astype(BF)
+
+    place[...] = one_hot(place.shape[0], 0)
+    own_place[...] = one_hot(capacity, at_ref[0] * capacity)
+    sent[...] = dot(own_place[...], tokens[...]).astype(BF)
+
+
+def routed(at, route, tokens, capacity, quarter):
+    rows = route.shape[1]
+    shapes = ((capacity, rows), (EXPERTS * capacity, rows), (capacity, quarter))
+    return pl.pallas_call(
+        route_kernel,
+        out_shape=[jax.ShapeDtypeStruct(shape, BF) for shape in shapes],
+        grid_spec=pltpu.PrefetchScalarGridSpec(
+            num_scalar_prefetch=1,
+            grid=(1,),
+            in_specs=[
+                pl.BlockSpec((1, rows), lambda i, at: (0, 0)),
+                pl.BlockSpec((rows, quarter), lambda i, at: (0, at[1])),
+            ],
+            out_specs=[pl.BlockSpec(shape, lambda i, at: (0, 0)) for shape in shapes],
+        ),
+        compiler_params=pltpu.CompilerParams(vmem_limit_bytes=32 * 1024 * 1024),
+        cost_estimate=pl.CostEstimate(flops=COST, bytes_accessed=COST, transcendentals=0),
+    )(at, route, tokens)
+
+
 def take_cols(value, index, width):
     return lax.dynamic_slice_in_dim(value, index * width, width, axis=1)
 
@@ -204,28 +262,20 @@
 
     def over_z(blocks):
         groups = [[2 * i + j for i in range(EXPERTS)] for j in range(2)]
-        got = lax.all_to_all(blocks, "owner", 0, 0, tiled=True, axis_index_groups=groups)
-        return got.reshape(EXPERTS, -1, part)
-
-    experts = jnp.arange(EXPERTS, dtype=jnp.int32)[:, None]
-    member = route.T == experts
-    rank = jnp.cumsum(member.astype(jnp.int32), axis=1) - 1
-    rank = jnp.sum(jnp.where(member, rank, 0), axis=0)
-    own_slot = jnp.where(route[:, 0] == z, rank, -1)
-    own_place = (own_slot[None, :] == jnp.arange(capacity, dtype=jnp.int32)[:, None]).astype(BF)
-    slot = rank + route[:, 0] * capacity
-    hot = slot[None, :] == jnp.arange(EXPERTS * capacity, dtype=jnp.int32)[:, None]
-    place = hot.astype(BF)
+        return lax.all_to_all(blocks, "owner", 0, 0, tiled=True, axis_index_groups=groups)
+
+    at = jnp.stack([z, d ^ (2 + x)])
+    own_place, place, x_sent = routed(at, route.reshape(1, rows), tokens, capacity, quarter)
 
     def x_cols(k):
         return take_cols(tokens, d ^ k, quarter)
 
-    x_sent = dot(own_place, x_cols(2 + x)).astype(BF)
     x_got = by_y(x_sent)
     x_own = [dot(own_place, x_cols(k)).astype(BF) for k in (0, 1)]
 
     d_expert = (gate_prob[:, None] * d_out.astype(F32)).astype(BF)
-    cot_got = over_z(dot(place, after(d_expert, x_sent)).astype(BF))
+    cot_sent = dot(place, after(d_expert, x_sent)).astype(BF)
+    cot_got = over_z(cot_sent.reshape(EXPERTS, capacity, part))
 
     core_gate, core_up, core_down = by_core(w_gate), by_core(w_up), by_core(w_down)
 
@@ -250,7 +300,6 @@
     cot_own_other = by_x(cot_own)
 
     x_got, x_other, _, _ = lax.optimization_barrier((x_got, x_other, cot_far, cot_own))
-    x_rem = [jnp.where(x == 0, x_got, x_other), jnp.where(x == 0, x_other, x_got)]
     part_rem, sent_rem = projected(x_at, x_got, x_other, COST)
     far_own = by_y(sent_rem)
 
@@ -289,10 +338,11 @@
 
     def plane_blocks(near, far, note=None):
         blocks = jnp.stack([near[:, :part], near[:, part:], far[:, :part], far[:, part:]])
-        sent = [lax.dynamic_index_in_dim(blocks, d ^ i, axis=0, keepdims=False) for i in range(EXPERTS)]
+        sent = [lax.dynamic_index_in_dim(blocks, d ^ i, axis=0, keepdims=True) for i in range(EXPERTS)]
+        sent = jnp.concatenate(sent, axis=0)
         if note is not None:
-            sent = [v for value in sent for v in (value, note)]
-        return jnp.concatenate(sent, axis=0)
+            sent = jnp.concatenate([sent, jnp.broadcast_to(note, (EXPERTS, *note.shape))], axis=1)
+        return sent
 
     def placed(got):
         return contract_rows(place, got[:, :capacity].reshape(EXPERTS * capacity, part))
@@ -310,12 +360,12 @@
     mine, other = output(hidden_rem)
     out_rem = added(mine, by_x(other))
     back_own, back_sent = back_of(cot_own, cot_own_other)
-    back_far_rem = by_y(back_sent)
+    back_far_rem = by_y(after(back_sent, out_rem))
     out_far = by_y(out_rem)
     cot_rem_other = by_x(cot_rem)
     out_mine, out_other = output(hidden_own)
     out_near = added(out_mine, by_x(out_other))
-    back_rem, back_sent = back_of(cot_rem, cot_rem_other)
+    back_rem, back_sent = back_of(cot_rem, after(cot_rem_other, back_far_rem))
     out_sent = plane_blocks(out_near, out_far)
     out_blocks = over_z(out_sent)
     back_far_own = by_y(after(back_sent, out_near))
@@ -324,40 +374,54 @@
     d_gate_rem, d_up_rem, _ = backward(pre_rem, back_rem, back_far_rem)
     d_gate_own, d_up_own, router = backward(pre_own, back_own, back_far_own)
     mine, other = d_input(d_gate_rem, d_up_rem)
-    in_far = by_y(added(mine, by_x(other)))
+    in_rem = added(mine, by_x(other))
+    in_far = by_y(in_rem)
+    back_far_own = after(back_far_own, in_rem)
     mine, other = d_input(d_gate_own, d_up_own)
     wide = jnp.pad(noted(router), ((0, 0), (0, other.shape[1] - part)))
     in_sent = jnp.concatenate([other, wide], axis=0)
     in_got = by_x(in_sent)
     in_near = added(mine, in_got[:capacity])
-    in_blocks = over_z(
-        plane_blocks(in_near, in_far, noted(router + read_note(in_got[capacity:])))
-    )
+    in_planes = plane_blocks(in_near, in_far, noted(router + read_note(in_got[capacity:])))
+    in_blocks = over_z(in_planes)
 
     notes = jnp.concatenate([read_note(v) for v in in_blocks[:, capacity:]])
-    grad_gate = jnp.sum(jnp.where(hot, notes[:, None], F32(0.0)), axis=0) / gate_prob
+    grad_gate = jnp.sum(place.astype(F32) * notes[:, None], axis=0) / gate_prob
     mixed = (gate_prob[:, None] * placed(out_blocks)).astype(BF)
     grad_tokens = placed(in_blocks).astype(BF)
 
-    d_gate_own, d_gate_rem, d_up_own, d_up_rem, _ = lax.optimization_barrier(
-        (d_gate_own, d_gate_rem, d_up_own, d_up_rem, in_sent)
-    )
-    hidden_own, hidden_rem, _ = lax.optimization_barrier((hidden_own, hidden_rem, in_sent))
-    x_keep, x_give = (jnp.concatenate([own, rem], axis=0) for own, rem in zip(x_own, x_rem))
-    mine_all = jnp.concatenate([cot_own, cot_rem], axis=0)
-    other_all = jnp.concatenate([cot_own_other, cot_rem_other], axis=0)
-    d_gate_all = jnp.concatenate([d_gate_own, d_gate_rem], axis=0)
-    d_up_all = jnp.concatenate([d_up_own, d_up_rem], axis=0)
-    hidden_all = jnp.concatenate([hidden_own, hidden_rem], axis=0)
+    def held(mark, *values):
+        return lax.optimization_barrier((*values, mark))[:-1]
+
+    def tall(own, rem):
+        return jnp.concatenate([own, rem], axis=0)
+
+    def down_term(mark, k):
+        hidden_1, hidden_2, mine_1, mine_2, other_1, other_2 = held(
+            mark, hidden_own, hidden_rem, cot_own, cot_rem, cot_own_other, cot_rem_other
+        )
+        at = slice(k * part, (k + 1) * part)
+        rows_mine, rows_other = tall(mine_1[:, at], mine_2[:, at]), tall(other_1[:, at], other_2[:, at])
+        return contract_rows(tall(hidden_1, hidden_2), jnp.concatenate([rows_mine, rows_other], axis=1))
+
+    def token_term(mark, k, own, rem):
+        x_1, got, other, grad_1, grad_2 = held(mark, x_own[k], x_got, x_other, own, rem)
+        x_2 = jnp.where(x == k, got, other)
+        return contract_rows(tall(x_1, x_2), tall(grad_1, grad_2))
 
     def in_chip(keep, give):
         return keep + by_core(give.astype(BF)).astype(F32)
 
-    grad_w_gate = in_chip(contract_rows(x_keep, d_gate_all), contract_rows(x_give, d_gate_all))
-    grad_w_up = in_chip(contract_rows(x_keep, d_up_all), contract_rows(x_give, d_up_all))
-    down_keep = jnp.concatenate([mine_all[:, :part], other_all[:, :part]], axis=1)
-    down_give = jnp.concatenate([mine_all[:, part:], other_all[:, part:]], axis=1)
-    grad_down = in_chip(contract_rows(hidden_all, down_keep), contract_rows(hidden_all, down_give))
+    grads_gate, grads_up = (d_gate_own, d_gate_rem), (d_up_own, d_up_rem)
+    terms = held(
+        in_sent, hidden_own, hidden_rem, cot_own, cot_rem, cot_own_other, cot_rem_other,
+        x_own[1], x_got, x_other, *grads_gate, *grads_up
+    )
+    outs = (((size, 2 * part), BF), ((quarter, size), BF), ((quarter, size), BF))
+    give_down, give_gate, give_up = on_core(terms_kernel, outs, x_at, *terms, cost=TERM_COST)
+    grad_w_gate = in_chip(token_term(in_planes, 0, *grads_gate), give_gate)
+    grad_w_up = in_chip(token_term(in_planes, 0, *grads_up), give_up)
+    grad_down = in_chip(down_term(in_planes, 0), give_down)
     turned = jnp.concatenate([grad_down[:, part:], grad_down[:, :part]], axis=1)
     grad_w_down = jnp.where(x == 0, grad_down, turned)
     return (mixed, grad_tokens, grad_gate, grad_w_gate, grad_w_up, grad_w_down)

time: 225 us -> 217 us (0.964)
  Pallas kernels: 21.6 us -> 38.9 us
  waiting for transfers between devices: 89.6 us -> 79.1 us
  matrix products: 32.6 us -> 23.3 us
  other arithmetic: 24.5 us -> 20.5 us
  local copies, waits for them, and re-layouts: 19.2 us -> 16.8 us
    pallas_call x8 -> x9, Pallas kernels: 21.6 us -> 36.1 us  [on_core(): pl.pallas_call(body, out_shape=[jax.ShapeDtypeStruct(shape, kind) for sha...]
    dot_general x8 -> x5, matrix products: 23.7 us -> 17.2 us  [contract_rows(): lax.dot_general(left, right, (((0,), (0,)), ((), ())), preferred_element_...]
    all_to_all x3, waiting for transfers between devices: 43.9 us -> 37.8 us  [over_z(): lax.all_to_all(blocks, 'owner', 0, 0, tiled=True, axis_index_groups=groups)]
    ppermute x21, waiting for transfers between devices: 45.8 us -> 41.4 us  [swap(): return lax.ppermute(value, axis, pairs)]
    pallas_call x0 -> x1, Pallas kernels: none -> 2.84 us  [routed(): pl.pallas_call(route_kernel, out_shape=[jax.ShapeDtypeStruct(shape, BF) f...]
    dot_general x4 -> x3, matrix products: 8.89 us -> 6.15 us  [dot(): return jnp.dot(left, right, preferred_element_type=jnp.float32)]
    slice x3 -> x6, local copies, waits for them, and re-layouts: 2.9 us -> 0.28 us  [the longest x2 0.12 us: down_term(): other_2[:, at]]
    unnamed x104 -> x114, local copies, waits for them, and re-layouts: 13.1 us -> 11.8 us
  transfers between devices with their start and end apart: 24 -> 24, of which waited for: 13 -> 11; matrix products, arithmetic and copies ran while one was open for 27% -> 20% of each run, Pallas kernels for 10% -> 18%
where the time goes in v3:
time: 217 us; the launch traced here: 216 us
  waiting for transfers between devices  79.1 us (36%)
  Pallas kernels  38.9 us (18%)
  starting transfers between devices  36.2 us (17%)
  matrix products  23.3 us (11%)
  other arithmetic  20.5 us (9%)
  local copies, waits for them, and re-layouts  16.8 us (8%)
    ppermute x21, waiting for transfers between devices, swap(): return lax.ppermute(value, axis, pairs)  41.4 us
    all_to_all x3, waiting for transfers between devices, over_z(): lax.all_to_all(blocks, 'owner', 0, 0, tiled=True, axis_index_groups=groups)  37.8 us
    pallas_call x9, Pallas kernels, on_core(): pl.pallas_call(body, out_shape=[jax.ShapeDtypeStruct(shape, kind) for sha...  36.1 us
    ppermute x21, starting transfers between devices, swap(): return lax.ppermute(value, axis, pairs)  22.2 us
    dot_general x5, matrix products, contract_rows(): lax.dot_general(left, right, (((0,), (0,)), ((), ())), preferred_element_...  17.2 us
    all_to_all x3, starting transfers between devices, over_z(): lax.all_to_all(blocks, 'owner', 0, 0, tiled=True, axis_index_groups=groups)  14.1 us
    unnamed x114, local copies, waits for them, and re-layouts  11.8 us
    dot_general x3, matrix products, dot(): return jnp.dot(left, right, preferred_element_type=jnp.float32)  6.15 us
  transfers between devices with their start and end apart: 24, of which 11 were waited for; matrix products, arithmetic and copies ran while one was open for 20% of the time, Pallas kernels for 18%

profile of v3, /device:TPU:0, one launch (start us, length us, event | category | flops | bytes accessed | tf_op | source)
XLA Modules:
  0.0 216.4 jit_solution(9808218985181294015)
XLA Ops:
  4.2 2.8 %shard_map.118 = (bf16[384,512]{1,0:T(8,128)(2,1)S(1)}, bf16[1536,512]{1,0:T(8,128)(2,1)S(1)}, bf16[384,1024]{1,0:T(8,128)(2,1)}) custom-call(s32[2]{0:T(128)S(1)} %pad_add_fusion.at_ref, s32[1,512]{1,0:T(1,128)S(1)} %bitcast.47, bf16[512,4096]{1,0:T(8,128)(2,1)S(1)} %copy-done.15), custom_call_target="tpu_custom_call" | custom-call | flops 1024 | bytes 1024 | tf_op jit(solution)/shard_map/pallas_call | solution.py:223
  7.0 2.9 %collective-permute-start.2 = (bf16[384,1024]{1,0:T(8,128)(2,1)}, bf16[384,1024]{1,0:T(8,128)(2,1)}, u32[]{:S(2)}, u32[]{:S(2)}) collective-permute-start(bf16[384,1024]{1,0:T(8,128)(2,1)} %get-tuple-element.81), channel_id=1, source_target_pairs={{0,16},{8,24},{16,0},{24,8},{1,17},{9,25},{17,1},{25,9},{2,18},{10... | collective-permute-start | bytes 2359304 | tf_op jit(solution)/shard_map/ppermute | solution.py:97
  12.3 4.9 %all-to-all-start = ((bf16[4,384,512]{2,1,0:T(8,128)(2,1)}), bf16[4,384,512]{2,1,0:T(8,128)(2,1)}, u32[]{:S(2)}, u32[]{:S(2)}) async-start(bf16[4,384,512]{2,1,0:T(8,128)(2,1)} %bitcast.49), calls=%async_computation | async-start | bytes 3145728 | tf_op jit(solution)/shard_map/all_to_all | solution.py:265
  21.3 5.9 %shard_map.119 = (f32[384,1536]{1,0:T(8,128)S(1)}, bf16[384,1536]{1,0:T(8,128)(2,1)}) custom-call(s32[1]{0:T(128)} %constant.69.clone.1.x_ref, bf16[384,1024]{1,0:T(8,128)(2,1)S(1)} %convolution_convert_fusion.2.first, bf16[384,1024]{1,0:T(8,128)(2,1)S(1)} %convolution_convert_fusion.1.second.tokens, bf16[1024,768]{1,0:T(8,128)(2,1)S(1)} %copy-done.3, ...), custom_call_target="tpu_custom_call" | custom-call | flops 20000000000 | bytes 1024 | tf_op jit(solution)/shard_map/pallas_call | solution.py:117
  31.3 22.9 %all-to-all-done = bf16[4,384,512]{2,1,0:T(8,128)(2,1)} async-done(((bf16[4,384,512]{2,1,0:T(8,128)(2,1)}), bf16[4,384,512]{2,1,0:T(8,128)(2,1)}, u32[]{:S(2)}, u32[]{:S(2)}) %all-to-all-start) | async-done | bytes 1572896 | tf_op jit(solution)/shard_map/all_to_all | solution.py:265
  58.9 4.5 %shard_map.120 = (f32[384,1536]{1,0:T(8,128)S(1)}, bf16[384,1536]{1,0:T(8,128)(2,1)S(1)}) custom-call(s32[1]{0:T(128)} %bitcast.3.x_ref, bf16[384,1024]{1,0:T(8,128)(2,1)} %collective-permute-done.2.first.got, bf16[384,1024]{1,0:T(8,128)(2,1)} %collective-permute-done.3.second.swapped, bf16[1024,768]{1,0:T(8,128)(2,1)S(1)} %copy-done.4, ...), custom_call_target="tpu_custom_call" | custom-call | flops 1024 | bytes 1024 | tf_op jit(solution)/shard_map/pallas_call | solution.py:117
  65.0 9.5 %collective-permute-done.5.mine.mine_rem = bf16[384,1024]{1,0:T(8,128)(2,1)S(1)} collective-permute-done((bf16[384,1024]{1,0:T(8,128)(2,1)S(1)}, bf16[384,1024]{1,0:T(8,128)(2,1)S(1)}, u32[]{:S(2)}, u32[]{:S(2)}) %collective-permute-start.5) | collective-permute-done | bytes 786464 | tf_op jit(solution)/shard_map/ppermute | solution.py:97
  80.6 13.9 %collective-permute-done.9 = bf16[384,1024]{1,0:T(8,128)(2,1)S(1)} collective-permute-done((bf16[384,1024]{1,0:T(8,128)(2,1)S(1)}, bf16[384,1024]{1,0:T(8,128)(2,1)S(1)}, u32[]{:S(2)}, u32[]{:S(2)}) %collective-permute-start.9) | collective-permute-done | bytes 786464 | tf_op jit(solution)/shard_map/ppermute | solution.py:97
  97.3 3.1 %collective-permute-done.6 = bf16[384,1536]{1,0:T(8,128)(2,1)S(1)} collective-permute-done((bf16[384,1536]{1,0:T(8,128)(2,1)S(1)}, bf16[384,1536]{1,0:T(8,128)(2,1)S(1)}, u32[]{:S(2)}, u32[]{:S(2)}) %collective-permute-start.6) | collective-permute-done | bytes 1179680 | tf_op jit(solution)/shard_map/ppermute | solution.py:97
  106.3 4.8 %collective-permute-done.10.other.other_rem = bf16[384,1024]{1,0:T(8,128)(2,1)S(1)} collective-permute-done((bf16[384,1024]{1,0:T(8,128)(2,1)S(1)}, bf16[384,1024]{1,0:T(8,128)(2,1)S(1)}, u32[]{:S(2)}, u32[]{:S(2)}) %collective-permute-start.10) | collective-permute-done | bytes 786464 | tf_op jit(solution)/shard_map/ppermute | solution.py:97
  117.3 2.5 %shard_map.124 = (f32[384,768]{1,0:T(8,128)S(1)}, bf16[384,768]{1,0:T(8,128)(2,1)}) custom-call(s32[1]{0:T(128)} %bitcast.3.x_ref, bf16[384,1024]{1,0:T(8,128)(2,1)S(1)} %copy-done.34, bf16[384,1024]{1,0:T(8,128)(2,1)S(1)} %copy-done.40, bf16[768,1024]{1,0:T(8,128)(2,1)S(1)} %copy-done, bf16[768,1024]{1,0:T(8,128)(2,1)S(1)} %collective-permute-done.7.core_down), custom_call_target="tpu_custom_call" | custom-call | flops 1024 | bytes 1024 | tf_op jit(solution)/shard_map/pallas_call | solution.py:117
  122.3 5.0 %shard_map.126 = (f32[384,1024]{1,0:T(8,128)S(1)}, bf16[384,1024]{1,0:T(8,128)(2,1)}) custom-call(s32[1]{0:T(128)} %bitcast.3.x_ref, bf16[384,768]{1,0:T(8,128)(2,1)S(1)} %get-tuple-element.122.d_gate.d_gate_rem, bf16[384,768]{1,0:T(8,128)(2,1)S(1)} %get-tuple-element.141.d_up.d_up_rem, bf16[1024,768]{1,0:T(8,128)(2,1)S(1)} %copy-done.5, ...), custom_call_target="tpu_custom_call" | custom-call | flops 1024 | bytes 1024 | tf_op jit(solution)/shard_map/pallas_call | solution.py:117
  136.0 4.5 %all-to-all-start.1 = ((bf16[4,384,512]{2,1,0:T(8,128)(2,1)}), bf16[4,384,512]{2,1,0:T(8,128)(2,1)}, u32[]{:S(2)}, u32[]{:S(2)}) async-start(bf16[4,384,512]{2,1,0:T(8,128)(2,1)} %pad_maximum_fusion.2), calls=%async_computation.1 | async-start | bytes 3145728 | tf_op jit(solution)/shard_map/all_to_all | solution.py:265
  140.5 3.7 %collective-permute-done.15 = bf16[384,1024]{1,0:T(8,128)(2,1)} collective-permute-done((bf16[384,1024]{1,0:T(8,128)(2,1)}, bf16[384,1024]{1,0:T(8,128)(2,1)}, u32[]{:S(2)}, u32[]{:S(2)}) %collective-permute-start.15) | collective-permute-done | bytes 786464 | tf_op jit(solution)/shard_map/ppermute | solution.py:97
  146.2 2.8 %multiply_convert_fusion.2 = (bf16[384,768]{1,0:T(8,128)(2,1)S(1)}, bf16[384,768]{1,0:T(8,128)(2,1)S(1)}, f32[384]{0:T(512)S(1)}) fusion(f32[384,768]{1,0:T(8,128)S(1)} %copy-done.46, bf16[384,768]{1,0:T(8,128)(2,1)} %collective-permute-done.14, f32[384,1536]{1,0:T(8,128)} %copy-done.52), kind=kLoop, calls=%fused_computation.52 | loop fusion | flops 5897856 | bytes 5309952 | tf_op jit(solution)/shard_map/convert_element_type | solution.py:321
  149.2 4.4 %shard_map.125 = (f32[384,1024]{1,0:T(8,128)S(1)}, bf16[384,1024]{1,0:T(8,128)(2,1)S(1)}) custom-call(s32[1]{0:T(128)} %bitcast.3.x_ref, bf16[384,768]{1,0:T(8,128)(2,1)S(1)} %get-tuple-element.121.d_gate, bf16[384,768]{1,0:T(8,128)(2,1)S(1)} %get-tuple-element.140.d_up, bf16[1024,768]{1,0:T(8,128)(2,1)S(1)} %copy-done.5, bf16[1024,768]{1,0:T(8,128)(2,1)S(1)} %copy-done.12, ...), custom_call_target="tpu_custom_call" | custom-call | flops 1024 | bytes 1024 | tf_op jit(solution)/shard_map/pallas_call | solution.py:117
  157.1 7.7 %shard_map.127 = (bf16[768,1024]{1,0:T(8,128)(2,1)}, bf16[1024,768]{1,0:T(8,128)(2,1)S(1)}, bf16[1024,768]{1,0:T(8,128)(2,1)}) custom-call(s32[1]{0:T(128)} %bitcast.3.x_ref, bf16[384,768]{1,0:T(8,128)(2,1)S(1)} %copy-done.21, bf16[384,768]{1,0:T(8,128)(2,1)S(1)} %copy-done.19, bf16[384,1024]{1,0:T(8,128)(2,1)S(1)} %copy-done.14, ...), custom_call_target="tpu_custom_call" | custom-call | flops 20000000000 | bytes 1024 | tf_op jit(solution)/shard_map/pallas_call | solution.py:117
  165.3 3.2 %collective-permute-done.17 = bf16[384,1024]{1,0:T(8,128)(2,1)S(1)} collective-permute-done((bf16[384,1024]{1,0:T(8,128)(2,1)S(1)}, bf16[384,1024]{1,0:T(8,128)(2,1)S(1)}, u32[]{:S(2)}, u32[]{:S(2)}) %collective-permute-start.17) | collective-permute-done | bytes 786464 | tf_op jit(solution)/shard_map/ppermute | solution.py:97
  170.6 4.6 %all-to-all-start.2 = ((bf16[4,400,512]{2,1,0:T(8,128)(2,1)}), bf16[4,400,512]{2,1,0:T(8,128)(2,1)}, u32[]{:S(2)}, u32[]{:S(2)}) async-start(bf16[4,400,512]{2,1,0:T(8,128)(2,1)} %pad_maximum_fusion), calls=%async_computation.2 | async-start | bytes 3276800 | tf_op jit(solution)/shard_map/all_to_all | solution.py:265
  178.1 2.8 %convert_add_fusion = f32[768,1024]{1,0:T(8,128)S(1)} fusion(bf16[768,1024]{1,0:T(8,128)(2,1)} %collective-permute-done.20, bf16[384,512]{1,0:T(8,128)(2,1)S(1)} %slice-done.1, bf16[384,512]{1,0:T(8,128)(2,1)S(1)} %slice-done, bf16[384,512]{1,0:T(8,128)(2,1)S(1)} %slice.102, bf16[384,512]{1,0:T(8,128)(2,1)S(1)} %slice.101, ...), kind=kOutput, calls=%fused_computation.1 | convolution fusion | flops 1218183168 | bytes 7471104 | tf_op jit(solution)/shard_map/dot_general | solution.py:18
  183.8 4.6 %convert_add_fusion.1 = f32[1024,768]{1,0:T(8,128)} fusion(bf16[1024,768]{1,0:T(8,128)(2,1)} %collective-permute-done.19, bf16[384,1024]{1,0:T(8,128)(2,1)S(1)} %get-tuple-element.191, bf16[384,1024]{1,0:T(8,128)(2,1)S(1)} %copy-done.49, bf16[384,768]{1,0:T(8,128)(2,1)S(1)} %copy-done.32, bf16[384,768]{1,0:T(8,128)(2,1)S(1)} %copy-done.26), kind=kOutput, calls=%fused_computation.2 | convolution fusion | flops 1215037440 | bytes 7471104 | tf_op jit(solution)/shard_map/dot_general | solution.py:18
  188.5 4.7 %convert_add_fusion.2 = f32[1024,768]{1,0:T(8,128)} fusion(bf16[1024,768]{1,0:T(8,128)(2,1)} %collective-permute-done.18, bf16[384,1024]{1,0:T(8,128)(2,1)S(1)} %get-tuple-element.192, bf16[384,1024]{1,0:T(8,128)(2,1)S(1)} %copy-done.49, bf16[384,768]{1,0:T(8,128)(2,1)S(1)} %copy-done.29, bf16[384,768]{1,0:T(8,128)(2,1)S(1)} %copy-done.24), kind=kOutput, calls=%fused_computation.3 | convolution fusion | flops 1215037440 | bytes 7471104 | tf_op jit(solution)/shard_map/dot_general | solution.py:18
  193.1 3.2 %fusion.23 = bf16[512,512]{1,0:T(8,128)(2,1)} fusion(bf16[1536,512]{1,0:T(8,128)(2,1)S(1)} %copy-done.2, bf16[1536,512]{1,0:T(8,128)(2,1)} %bitcast.13, f32[512]{0:T(512)S(1)} %copy-done.56), kind=kOutput, calls=%fused_computation.38 | convolution fusion | flops 805830656 | bytes 3672064 | tf_op jit(solution)/shard_map/dot_general | solution.py:18
  196.3 14.9 %all-to-all-done.2 = bf16[4,400,512]{2,1,0:T(8,128)(2,1)} async-done(((bf16[4,400,512]{2,1,0:T(8,128)(2,1)}), bf16[4,400,512]{2,1,0:T(8,128)(2,1)}, u32[]{:S(2)}, u32[]{:S(2)}) %all-to-all-start.2) | async-done | bytes 1638432 | tf_op jit(solution)/shard_map/all_to_all | solution.py:265
  (206 shorter events, 70.8 us)
Async XLA Ops:
  0.6 20.6 %collective-permute-start = (bf16[1024,768]{1,0:T(8,128)(2,1)}, bf16[1024,768]{1,0:T(8,128)(2,1)S(1)}, u32[]{:S(2)}, u32[]{:S(2)}) collective-permute-start(bf16[1024,768]{1,0:T(8,128)(2,1)} %gate.7), channel_id=1, source_target_pairs={{0,8},{8,0},{16,24},{24,16},{1,9},{9,1},{17,25},{25,17},{2,10},{10... | collective-permute-start | bytes 4718600 | tf_op jit(solution)/shard_map/ppermute | solution.py:97
  1.1 20.1 %collective-permute-start.1 = (bf16[1024,768]{1,0:T(8,128)(2,1)}, bf16[1024,768]{1,0:T(8,128)(2,1)}, u32[]{:S(2)}, u32[]{:S(2)}) collective-permute-start(bf16[1024,768]{1,0:T(8,128)(2,1)} %up.7), channel_id=1, source_target_pairs={{0,8},{8,0},{16,24},{24,16},{1,9},{9,1},{17,25},{25,17},{2,10},{10... | collective-permute-start | bytes 4718600 | tf_op jit(solution)/shard_map/ppermute | solution.py:97
  7.0 21.6 %collective-permute-start.2 = (bf16[384,1024]{1,0:T(8,128)(2,1)}, bf16[384,1024]{1,0:T(8,128)(2,1)}, u32[]{:S(2)}, u32[]{:S(2)}) collective-permute-start(bf16[384,1024]{1,0:T(8,128)(2,1)} %get-tuple-element.81), channel_id=1, source_target_pairs={{0,16},{8,24},{16,0},{24,8},{1,17},{9,25},{17,1},{25,9},{2,18},{10... | collective-permute-start | bytes 2359304 | tf_op jit(solution)/shard_map/ppermute | solution.py:97
  12.3 41.9 %all-to-all-start = ((bf16[4,384,512]{2,1,0:T(8,128)(2,1)}), bf16[4,384,512]{2,1,0:T(8,128)(2,1)}, u32[]{:S(2)}, u32[]{:S(2)}) async-start(bf16[4,384,512]{2,1,0:T(8,128)(2,1)} %bitcast.49), calls=%async_computation | async-start | bytes 3145728 | tf_op jit(solution)/shard_map/all_to_all | solution.py:265
  28.6 27.7 %collective-permute-start.4 = (bf16[384,1536]{1,0:T(8,128)(2,1)}, bf16[384,1536]{1,0:T(8,128)(2,1)}, u32[]{:S(2)}, u32[]{:S(2)}) collective-permute-start(bf16[384,1536]{1,0:T(8,128)(2,1)} %get-tuple-element.88), channel_id=1, source_target_pairs={{0,16},{8,24},{16,0},{24,8},{1,17},{9,25},{17,1},{25,9},{2,18},{10... | collective-permute-start | bytes 3538952 | tf_op jit(solution)/shard_map/ppermute | solution.py:97
  29.8 27.5 %collective-permute-start.3 = (bf16[384,1024]{1,0:T(8,128)(2,1)}, bf16[384,1024]{1,0:T(8,128)(2,1)}, u32[]{:S(2)}, u32[]{:S(2)}) collective-permute-start(bf16[384,1024]{1,0:T(8,128)(2,1)} %collective-permute-done.2.first.got), channel_id=1, source_target_pairs={{0,1},{1,0},{2,3},{3,2},{4,5},{5,4},{6,7},{7,6},{8,9},{9,8},{10,11... | collective-permute-start | bytes 2359304 | tf_op jit(solution)/shard_map/ppermute | solution.py:97
  31.3 44.0 %collective-permute-start.7 = (bf16[768,1024]{1,0:T(8,128)(2,1)S(1)}, bf16[768,1024]{1,0:T(8,128)(2,1)S(1)}, u32[]{:S(2)}, u32[]{:S(2)}) collective-permute-start(bf16[768,1024]{1,0:T(8,128)(2,1)S(1)} %copy-done), channel_id=1, source_target_pairs={{0,8},{8,0},{16,24},{24,16},{1,9},{9,1},{17,25},{25,17},{2,10},{10... | collective-permute-start | bytes 4718600 | tf_op jit(solution)/shard_map/ppermute | solution.py:97
  56.3 18.1 %collective-permute-start.5 = (bf16[384,1024]{1,0:T(8,128)(2,1)S(1)}, bf16[384,1024]{1,0:T(8,128)(2,1)S(1)}, u32[]{:S(2)}, u32[]{:S(2)}) collective-permute-start(bf16[384,1024]{1,0:T(8,128)(2,1)S(1)} %pad_maximum_fusion.4), channel_id=1, source_target_pairs={{0,16},{8,24},{16,0},{24,8},{1,17},{9,25},{17,1},{25,9},{2,18},{10... | collective-permute-start | bytes 2359304 | tf_op jit(solution)/shard_map/ppermute | solution.py:97
  57.3 19.5 %collective-permute-start.8 = (bf16[384,1024]{1,0:T(8,128)(2,1)S(1)}, bf16[384,1024]{1,0:T(8,128)(2,1)S(1)}, u32[]{:S(2)}, u32[]{:S(2)}) collective-permute-start(bf16[384,1024]{1,0:T(8,128)(2,1)S(1)} %pad_maximum_fusion.5.mine), channel_id=1, source_target_pairs={{0,1},{1,0},{2,3},{3,2},{4,5},{5,4},{6,7},{7,6},{8,9},{9,8},{10,11... | collective-permute-start | bytes 2359304 | tf_op jit(solution)/shard_map/ppermute | solution.py:97
  74.5 25.9 %collective-permute-start.6 = (bf16[384,1536]{1,0:T(8,128)(2,1)S(1)}, bf16[384,1536]{1,0:T(8,128)(2,1)S(1)}, u32[]{:S(2)}, u32[]{:S(2)}) collective-permute-start(bf16[384,1536]{1,0:T(8,128)(2,1)S(1)} %get-tuple-element.90), channel_id=1, source_target_pairs={{0,16},{8,24},{16,0},{24,8},{1,17},{9,25},{17,1},{25,9},{2,18},{10... | collective-permute-start | bytes 3538952 | tf_op jit(solution)/shard_map/ppermute | solution.py:97
  76.8 17.8 %collective-permute-start.9 = (bf16[384,1024]{1,0:T(8,128)(2,1)S(1)}, bf16[384,1024]{1,0:T(8,128)(2,1)S(1)}, u32[]{:S(2)}, u32[]{:S(2)}) collective-permute-start(bf16[384,1024]{1,0:T(8,128)(2,1)S(1)} %get-tuple-element.96), channel_id=1, source_target_pairs={{0,1},{1,0},{2,3},{3,2},{4,5},{5,4},{6,7},{7,6},{8,9},{9,8},{10,11... | collective-permute-start | bytes 2359304 | tf_op jit(solution)/shard_map/ppermute | solution.py:97
  94.6 16.5 %collective-permute-start.10 = (bf16[384,1024]{1,0:T(8,128)(2,1)S(1)}, bf16[384,1024]{1,0:T(8,128)(2,1)S(1)}, u32[]{:S(2)}, u32[]{:S(2)}) collective-permute-start(bf16[384,1024]{1,0:T(8,128)(2,1)S(1)} %collective-permute-done.5.mine.mine_rem), channel_id=1, source_target_pairs={{0,1},{1,0},{2,3},{3,2},{4,5},{5,4},{6,7},{7,6},{8,9},{9,8},{10,11... | collective-permute-start | bytes 2359304 | tf_op jit(solution)/shard_map/ppermute | solution.py:97
  100.4 13.5 %collective-permute-start.12 = (bf16[384,768]{1,0:T(8,128)(2,1)}, bf16[384,768]{1,0:T(8,128)(2,1)}, u32[]{:S(2)}, u32[]{:S(2)}) collective-permute-start(bf16[384,768]{1,0:T(8,128)(2,1)} %get-tuple-element.102), channel_id=1, source_target_pairs={{0,16},{8,24},{16,0},{24,8},{1,17},{9,25},{17,1},{25,9},{2,18},{10... | collective-permute-start | bytes 1769480 | tf_op jit(solution)/shard_map/ppermute | solution.py:97
  112.0 17.6 %collective-permute-start.11 = (bf16[384,1024]{1,0:T(8,128)(2,1)}, bf16[384,1024]{1,0:T(8,128)(2,1)}, u32[]{:S(2)}, u32[]{:S(2)}) collective-permute-start(bf16[384,1024]{1,0:T(8,128)(2,1)} %get-tuple-element.98), channel_id=1, source_target_pairs={{0,1},{1,0},{2,3},{3,2},{4,5},{5,4},{6,7},{7,6},{8,9},{9,8},{10,11... | collective-permute-start | bytes 2359304 | tf_op jit(solution)/shard_map/ppermute | solution.py:97
  113.9 18.8 %collective-permute-start.13 = (bf16[384,1024]{1,0:T(8,128)(2,1)}, bf16[384,1024]{1,0:T(8,128)(2,1)S(1)}, u32[]{:S(2)}, u32[]{:S(2)}) collective-permute-start(bf16[384,1024]{1,0:T(8,128)(2,1)} %add_convert_fusion.2), channel_id=1, source_target_pairs={{0,16},{8,24},{16,0},{24,8},{1,17},{9,25},{17,1},{25,9},{2,18},{10... | collective-permute-start | bytes 2359304 | tf_op jit(solution)/shard_map/ppermute | solution.py:97
  129.6 14.6 %collective-permute-start.15 = (bf16[384,1024]{1,0:T(8,128)(2,1)}, bf16[384,1024]{1,0:T(8,128)(2,1)}, u32[]{:S(2)}, u32[]{:S(2)}) collective-permute-start(bf16[384,1024]{1,0:T(8,128)(2,1)} %get-tuple-element.114), channel_id=1, source_target_pairs={{0,1},{1,0},{2,3},{3,2},{4,5},{5,4},{6,7},{7,6},{8,9},{9,8},{10,11... | collective-permute-start | bytes 2359304 | tf_op jit(solution)/shard_map/ppermute | solution.py:97
  132.7 13.5 %collective-permute-start.14 = (bf16[384,768]{1,0:T(8,128)(2,1)}, bf16[384,768]{1,0:T(8,128)(2,1)}, u32[]{:S(2)}, u32[]{:S(2)}) collective-permute-start(bf16[384,768]{1,0:T(8,128)(2,1)} %get-tuple-element.108), channel_id=1, source_target_pairs={{0,16},{8,24},{16,0},{24,8},{1,17},{9,25},{17,1},{25,9},{2,18},{10... | collective-permute-start | bytes 1769480 | tf_op jit(solution)/shard_map/ppermute | solution.py:97
  136.0 34.7 %all-to-all-start.1 = ((bf16[4,384,512]{2,1,0:T(8,128)(2,1)}), bf16[4,384,512]{2,1,0:T(8,128)(2,1)}, u32[]{:S(2)}, u32[]{:S(2)}) async-start(bf16[4,384,512]{2,1,0:T(8,128)(2,1)} %pad_maximum_fusion.2), calls=%async_computation.1 | async-start | bytes 3145728 | tf_op jit(solution)/shard_map/all_to_all | solution.py:265
  153.7 14.9 %collective-permute-start.16 = (bf16[400,1024]{1,0:T(8,128)(2,1)S(1)}, bf16[400,1024]{1,0:T(8,128)(2,1)S(1)}, u32[]{:S(2)}, u32[]{:S(2)}) collective-permute-start(bf16[400,1024]{1,0:T(8,128)(2,1)S(1)} %fusion.37), channel_id=1, source_target_pairs={{0,1},{1,0},{2,3},{3,2},{4,5},{5,4},{6,7},{7,6},{8,9},{9,8},{10,11... | collective-permute-start | bytes 2457608 | tf_op jit(solution)/shard_map/ppermute | solution.py:97
  155.2 13.3 %collective-permute-start.17 = (bf16[384,1024]{1,0:T(8,128)(2,1)S(1)}, bf16[384,1024]{1,0:T(8,128)(2,1)S(1)}, u32[]{:S(2)}, u32[]{:S(2)}) collective-permute-start(bf16[384,1024]{1,0:T(8,128)(2,1)S(1)} %add_convert_fusion), channel_id=1, source_target_pairs={{0,16},{8,24},{16,0},{24,8},{1,17},{9,25},{17,1},{25,9},{2,18},{10... | collective-permute-start | bytes 2359304 | tf_op jit(solution)/shard_map/ppermute | solution.py:97
  164.8 12.1 %collective-permute-start.20 = (bf16[768,1024]{1,0:T(8,128)(2,1)}, bf16[768,1024]{1,0:T(8,128)(2,1)}, u32[]{:S(2)}, u32[]{:S(2)}) collective-permute-start(bf16[768,1024]{1,0:T(8,128)(2,1)} %get-tuple-element.149), channel_id=1, source_target_pairs={{0,8},{8,0},{16,24},{24,16},{1,9},{9,1},{17,25},{25,17},{2,10},{10... | collective-permute-start | bytes 4718600 | tf_op jit(solution)/shard_map/ppermute | solution.py:97
  164.8 18.9 %collective-permute-start.19 = (bf16[1024,768]{1,0:T(8,128)(2,1)}, bf16[1024,768]{1,0:T(8,128)(2,1)}, u32[]{:S(2)}, u32[]{:S(2)}) collective-permute-start(bf16[1024,768]{1,0:T(8,128)(2,1)} %get-tuple-element.142), channel_id=1, source_target_pairs={{0,8},{8,0},{16,24},{24,16},{1,9},{9,1},{17,25},{25,17},{2,10},{10... | collective-permute-start | bytes 4718600 | tf_op jit(solution)/shard_map/ppermute | solution.py:97
  165.3 23.1 %collective-permute-start.18 = (bf16[1024,768]{1,0:T(8,128)(2,1)S(1)}, bf16[1024,768]{1,0:T(8,128)(2,1)}, u32[]{:S(2)}, u32[]{:S(2)}) collective-permute-start(bf16[1024,768]{1,0:T(8,128)(2,1)S(1)} %get-tuple-element.136), channel_id=1, source_target_pairs={{0,8},{8,0},{16,24},{24,16},{1,9},{9,1},{17,25},{25,17},{2,10},{10... | collective-permute-start | bytes 4718600 | tf_op jit(solution)/shard_map/ppermute | solution.py:97
  170.6 40.6 %all-to-all-start.2 = ((bf16[4,400,512]{2,1,0:T(8,128)(2,1)}), bf16[4,400,512]{2,1,0:T(8,128)(2,1)}, u32[]{:S(2)}, u32[]{:S(2)}) async-start(bf16[4,400,512]{2,1,0:T(8,128)(2,1)} %pad_maximum_fusion), calls=%async_computation.2 | async-start | bytes 3276800 | tf_op jit(solution)/shard_map/all_to_all | solution.py:265
  (59 other events, 298.5 us)

commit v4 on v3

--- a/solution.py
+++ b/solution.py
@@ -9,7 +9,7 @@
 XDEPTH = 1
 COST = 1024
 OWN_COST = 20 * 10**9
-TERM_COST = 20 * 10**9
+TERM_COST = 8 * 10**9
 BF = jnp.bfloat16
 F32 = jnp.float32
 
@@ -149,7 +149,7 @@
                 return weight[:, pl.ds(pl.multiple_of(half * part + j, BLOCK), BLOCK)]
 
             at = slice(k * part + j, k * part + j + BLOCK)
-            mine[:, at] = dot(hidden[...], cols(x))
+            mine[:, at] = dot(hidden[...], cols(x)).astype(BF)
             other[:, at] = dot(hidden[...], cols(1 - x)).astype(BF)
 
 
@@ -176,7 +176,7 @@
                 return contract_cols(d_gate[...], gate_k[at, :]) + contract_cols(d_up[...], up_k[at, :])
 
             at = slice(k * part + j, k * part + j + BLOCK)
-            mine[:, at] = value(x)
+            mine[:, at] = value(x).astype(BF)
             other[:, at] = value(1 - x).astype(BF)
 
 
@@ -325,16 +325,16 @@
     hidden_own, hidden_rem = pre_own[-1], pre_rem[-1]
 
     def added(mine, got):
-        return (mine + got.astype(F32)).astype(BF)
+        return (mine.astype(F32) + got.astype(F32)).astype(BF)
 
     def output(hidden):
         shape = (capacity, 2 * part)
-        return on_core(output_kernel, ((shape, F32), (shape, BF)), x_at, hidden, w_down, core_down)
+        return on_core(output_kernel, ((shape, BF), (shape, BF)), x_at, hidden, w_down, core_down)
 
     def d_input(d_gate, d_up):
         weights = (w_gate, core_gate, w_up, core_up)
         shape = (capacity, 2 * part)
-        return on_core(input_kernel, ((shape, F32), (shape, BF)), x_at, d_gate, d_up, *weights)
+        return on_core(input_kernel, ((shape, BF), (shape, BF)), x_at, d_gate, d_up, *weights)
 
     def plane_blocks(near, far, note=None):
         blocks = jnp.stack([near[:, :part], near[:, part:], far[:, :part], far[:, part:]])

time: 217 us -> 217 us (level)
  no operation moved by 1% of the time
where the time goes in v4:
time: 217 us; the launch traced here: 216 us
  waiting for transfers between devices  79.4 us (37%)
  Pallas kernels  38.8 us (18%)
  starting transfers between devices  36.1 us (17%)
  matrix products  23.3 us (11%)
  other arithmetic  20.3 us (9%)
  local copies, waits for them, and re-layouts  16.5 us (8%)
    ppermute x21, waiting for transfers between devices, swap(): return lax.ppermute(value, axis, pairs)  42.5 us
    all_to_all x3, waiting for transfers between devices, over_z(): lax.all_to_all(blocks, 'owner', 0, 0, tiled=True, axis_index_groups=groups)  36.9 us
    pallas_call x9, Pallas kernels, on_core(): pl.pallas_call(body, out_shape=[jax.ShapeDtypeStruct(shape, kind) for sha...  35.9 us
    ppermute x21, starting transfers between devices, swap(): return lax.ppermute(value, axis, pairs)  22.1 us
    dot_general x5, matrix products, contract_rows(): lax.dot_general(left, right, (((0,), (0,)), ((), ())), preferred_element_...  17.2 us
    all_to_all x3, starting transfers between devices, over_z(): lax.all_to_all(blocks, 'owner', 0, 0, tiled=True, axis_index_groups=groups)  14 us
    unnamed x114, local copies, waits for them, and re-layouts  11.5 us
    dot_general x3, matrix products, dot(): return jnp.dot(left, right, preferred_element_type=jnp.float32)  6.15 us
  transfers between devices with their start and end apart: 24, of which 11 were waited for; matrix products, arithmetic and copies ran while one was open for 20% of the time, Pallas kernels for 18%

profile of v4, /device:TPU:0, one launch (start us, length us, event | category | flops | bytes accessed | tf_op | source)
XLA Modules:
  0.0 215.9 jit_solution(160132337690317672)
XLA Ops:
  4.2 2.9 %shard_map.118 = (bf16[384,512]{1,0:T(8,128)(2,1)S(1)}, bf16[1536,512]{1,0:T(8,128)(2,1)S(1)}, bf16[384,1024]{1,0:T(8,128)(2,1)}) custom-call(s32[2]{0:T(128)S(1)} %pad_add_fusion.at_ref, s32[1,512]{1,0:T(1,128)S(1)} %bitcast.47, bf16[512,4096]{1,0:T(8,128)(2,1)S(1)} %copy-done.15), custom_call_target="tpu_custom_call" | custom-call | flops 1024 | bytes 1024 | tf_op jit(solution)/shard_map/pallas_call | solution.py:223
  7.0 2.9 %collective-permute-start.2 = (bf16[384,1024]{1,0:T(8,128)(2,1)}, bf16[384,1024]{1,0:T(8,128)(2,1)}, u32[]{:S(2)}, u32[]{:S(2)}) collective-permute-start(bf16[384,1024]{1,0:T(8,128)(2,1)} %get-tuple-element.81), channel_id=1, source_target_pairs={{0,16},{8,24},{16,0},{24,8},{1,17},{9,25},{17,1},{25,9},{2,18},{10... | collective-permute-start | bytes 2359304 | tf_op jit(solution)/shard_map/ppermute | solution.py:97
  12.3 4.9 %all-to-all-start = ((bf16[4,384,512]{2,1,0:T(8,128)(2,1)}), bf16[4,384,512]{2,1,0:T(8,128)(2,1)}, u32[]{:S(2)}, u32[]{:S(2)}) async-start(bf16[4,384,512]{2,1,0:T(8,128)(2,1)} %bitcast.49), calls=%async_computation | async-start | bytes 3145728 | tf_op jit(solution)/shard_map/all_to_all | solution.py:265
  21.3 6.0 %shard_map.119 = (f32[384,1536]{1,0:T(8,128)S(1)}, bf16[384,1536]{1,0:T(8,128)(2,1)}) custom-call(s32[1]{0:T(128)} %constant.69.clone.1.x_ref, bf16[384,1024]{1,0:T(8,128)(2,1)S(1)} %convolution_convert_fusion.2.first, bf16[384,1024]{1,0:T(8,128)(2,1)S(1)} %convolution_convert_fusion.1.second.tokens, bf16[1024,768]{1,0:T(8,128)(2,1)S(1)} %copy-done.3, ...), custom_call_target="tpu_custom_call" | custom-call | flops 20000000000 | bytes 1024 | tf_op jit(solution)/shard_map/pallas_call | solution.py:117
  31.3 22.9 %all-to-all-done = bf16[4,384,512]{2,1,0:T(8,128)(2,1)} async-done(((bf16[4,384,512]{2,1,0:T(8,128)(2,1)}), bf16[4,384,512]{2,1,0:T(8,128)(2,1)}, u32[]{:S(2)}, u32[]{:S(2)}) %all-to-all-start) | async-done | bytes 1572896 | tf_op jit(solution)/shard_map/all_to_all | solution.py:265
  58.9 4.5 %shard_map.120 = (f32[384,1536]{1,0:T(8,128)S(1)}, bf16[384,1536]{1,0:T(8,128)(2,1)S(1)}) custom-call(s32[1]{0:T(128)} %bitcast.3.x_ref, bf16[384,1024]{1,0:T(8,128)(2,1)} %collective-permute-done.2.first.got, bf16[384,1024]{1,0:T(8,128)(2,1)} %collective-permute-done.3.second.swapped, bf16[1024,768]{1,0:T(8,128)(2,1)S(1)} %copy-done.4, ...), custom_call_target="tpu_custom_call" | custom-call | flops 1024 | bytes 1024 | tf_op jit(solution)/shard_map/pallas_call | solution.py:117
  65.0 9.5 %collective-permute-done.5.mine.mine_rem = bf16[384,1024]{1,0:T(8,128)(2,1)S(1)} collective-permute-done((bf16[384,1024]{1,0:T(8,128)(2,1)S(1)}, bf16[384,1024]{1,0:T(8,128)(2,1)S(1)}, u32[]{:S(2)}, u32[]{:S(2)}) %collective-permute-start.5) | collective-permute-done | bytes 786464 | tf_op jit(solution)/shard_map/ppermute | solution.py:97
  80.7 13.9 %collective-permute-done.9 = bf16[384,1024]{1,0:T(8,128)(2,1)S(1)} collective-permute-done((bf16[384,1024]{1,0:T(8,128)(2,1)S(1)}, bf16[384,1024]{1,0:T(8,128)(2,1)S(1)}, u32[]{:S(2)}, u32[]{:S(2)}) %collective-permute-start.9) | collective-permute-done | bytes 786464 | tf_op jit(solution)/shard_map/ppermute | solution.py:97
  97.3 3.1 %collective-permute-done.6 = bf16[384,1536]{1,0:T(8,128)(2,1)S(1)} collective-permute-done((bf16[384,1536]{1,0:T(8,128)(2,1)S(1)}, bf16[384,1536]{1,0:T(8,128)(2,1)S(1)}, u32[]{:S(2)}, u32[]{:S(2)}) %collective-permute-start.6) | collective-permute-done | bytes 1179680 | tf_op jit(solution)/shard_map/ppermute | solution.py:97
  106.1 5.0 %collective-permute-done.10.other.other_rem = bf16[384,1024]{1,0:T(8,128)(2,1)S(1)} collective-permute-done((bf16[384,1024]{1,0:T(8,128)(2,1)S(1)}, bf16[384,1024]{1,0:T(8,128)(2,1)S(1)}, u32[]{:S(2)}, u32[]{:S(2)}) %collective-permute-start.10) | collective-permute-done | bytes 786464 | tf_op jit(solution)/shard_map/ppermute | solution.py:97
  117.3 2.5 %shard_map.124 = (f32[384,768]{1,0:T(8,128)S(1)}, bf16[384,768]{1,0:T(8,128)(2,1)}) custom-call(s32[1]{0:T(128)} %bitcast.3.x_ref, bf16[384,1024]{1,0:T(8,128)(2,1)S(1)} %copy-done.34, bf16[384,1024]{1,0:T(8,128)(2,1)S(1)} %copy-done.40, bf16[768,1024]{1,0:T(8,128)(2,1)S(1)} %copy-done, bf16[768,1024]{1,0:T(8,128)(2,1)S(1)} %collective-permute-done.7.core_down), custom_call_target="tpu_custom_call" | custom-call | flops 1024 | bytes 1024 | tf_op jit(solution)/shard_map/pallas_call | solution.py:117
  122.3 5.0 %shard_map.126 = (bf16[384,1024]{1,0:T(8,128)(2,1)S(1)}, bf16[384,1024]{1,0:T(8,128)(2,1)}) custom-call(s32[1]{0:T(128)} %bitcast.3.x_ref, bf16[384,768]{1,0:T(8,128)(2,1)S(1)} %get-tuple-element.122.d_gate.d_gate_rem, bf16[384,768]{1,0:T(8,128)(2,1)S(1)} %get-tuple-element.141.d_up.d_up_rem, bf16[1024,768]{1,0:T(8,128)(2,1)S(1)} %copy-done.5, ...), custom_call_target="tpu_custom_call" | custom-call | flops 1024 | bytes 1024 | tf_op jit(solution)/shard_map/pallas_call | solution.py:117
  136.0 4.5 %all-to-all-start.1 = ((bf16[4,384,512]{2,1,0:T(8,128)(2,1)}), bf16[4,384,512]{2,1,0:T(8,128)(2,1)}, u32[]{:S(2)}, u32[]{:S(2)}) async-start(bf16[4,384,512]{2,1,0:T(8,128)(2,1)} %pad_maximum_fusion.2), calls=%async_computation.1 | async-start | bytes 3145728 | tf_op jit(solution)/shard_map/all_to_all | solution.py:265
  140.6 3.6 %collective-permute-done.15 = bf16[384,1024]{1,0:T(8,128)(2,1)} collective-permute-done((bf16[384,1024]{1,0:T(8,128)(2,1)}, bf16[384,1024]{1,0:T(8,128)(2,1)}, u32[]{:S(2)}, u32[]{:S(2)}) %collective-permute-start.15) | collective-permute-done | bytes 786464 | tf_op jit(solution)/shard_map/ppermute | solution.py:97
  145.9 2.8 %multiply_convert_fusion.2 = (bf16[384,768]{1,0:T(8,128)(2,1)S(1)}, bf16[384,768]{1,0:T(8,128)(2,1)S(1)}, f32[384]{0:T(512)S(1)}) fusion(f32[384,768]{1,0:T(8,128)S(1)} %copy-done.43, bf16[384,768]{1,0:T(8,128)(2,1)} %collective-permute-done.14, f32[384,1536]{1,0:T(8,128)} %copy-done.52), kind=kLoop, calls=%fused_computation.52 | loop fusion | flops 5897856 | bytes 5309952 | tf_op jit(solution)/shard_map/convert_element_type | solution.py:321
  150.7 4.2 %shard_map.125 = (bf16[384,1024]{1,0:T(8,128)(2,1)S(1)}, bf16[384,1024]{1,0:T(8,128)(2,1)S(1)}) custom-call(s32[1]{0:T(128)} %bitcast.3.x_ref, bf16[384,768]{1,0:T(8,128)(2,1)S(1)} %get-tuple-element.121.d_gate, bf16[384,768]{1,0:T(8,128)(2,1)S(1)} %get-tuple-element.140.d_up, bf16[1024,768]{1,0:T(8,128)(2,1)S(1)} %copy-done.5, ...), custom_call_target="tpu_custom_call" | custom-call | flops 1024 | bytes 1024 | tf_op jit(solution)/shard_map/pallas_call | solution.py:117
  156.6 7.7 %shard_map.127 = (bf16[768,1024]{1,0:T(8,128)(2,1)}, bf16[1024,768]{1,0:T(8,128)(2,1)S(1)}, bf16[1024,768]{1,0:T(8,128)(2,1)}) custom-call(s32[1]{0:T(128)} %bitcast.3.x_ref, bf16[384,768]{1,0:T(8,128)(2,1)S(1)} %copy-done.21, bf16[384,768]{1,0:T(8,128)(2,1)S(1)} %copy-done.19, bf16[384,1024]{1,0:T(8,128)(2,1)S(1)} %copy-done.14, ...), custom_call_target="tpu_custom_call" | custom-call | flops 8000000000 | bytes 1024 | tf_op jit(solution)/shard_map/pallas_call | solution.py:117
  164.9 4.0 %collective-permute-done.16 = bf16[400,1024]{1,0:T(8,128)(2,1)S(1)} collective-permute-done((bf16[400,1024]{1,0:T(8,128)(2,1)S(1)}, bf16[400,1024]{1,0:T(8,128)(2,1)S(1)}, u32[]{:S(2)}, u32[]{:S(2)}) %collective-permute-start.16) | collective-permute-done | bytes 819232 | tf_op jit(solution)/shard_map/ppermute | solution.py:97
  171.0 4.6 %all-to-all-start.2 = ((bf16[4,400,512]{2,1,0:T(8,128)(2,1)}), bf16[4,400,512]{2,1,0:T(8,128)(2,1)}, u32[]{:S(2)}, u32[]{:S(2)}) async-start(bf16[4,400,512]{2,1,0:T(8,128)(2,1)} %pad_maximum_fusion), calls=%async_computation.2 | async-start | bytes 3276800 | tf_op jit(solution)/shard_map/all_to_all | solution.py:265
  178.5 2.8 %convert_add_fusion = f32[768,1024]{1,0:T(8,128)S(1)} fusion(bf16[768,1024]{1,0:T(8,128)(2,1)} %collective-permute-done.20, bf16[384,512]{1,0:T(8,128)(2,1)S(1)} %slice-done.1, bf16[384,512]{1,0:T(8,128)(2,1)S(1)} %slice-done, bf16[384,512]{1,0:T(8,128)(2,1)S(1)} %slice.102, bf16[384,512]{1,0:T(8,128)(2,1)S(1)} %slice.101, ...), kind=kOutput, calls=%fused_computation.1 | convolution fusion | flops 1218183168 | bytes 7471104 | tf_op jit(solution)/shard_map/dot_general | solution.py:18
  184.1 4.6 %convert_add_fusion.1 = f32[1024,768]{1,0:T(8,128)} fusion(bf16[1024,768]{1,0:T(8,128)(2,1)} %collective-permute-done.19, bf16[384,1024]{1,0:T(8,128)(2,1)S(1)} %get-tuple-element.191, bf16[384,1024]{1,0:T(8,128)(2,1)S(1)} %copy-done.49, bf16[384,768]{1,0:T(8,128)(2,1)S(1)} %copy-done.32, bf16[384,768]{1,0:T(8,128)(2,1)S(1)} %copy-done.26), kind=kOutput, calls=%fused_computation.2 | convolution fusion | flops 1215037440 | bytes 7471104 | tf_op jit(solution)/shard_map/dot_general | solution.py:18
  188.8 4.7 %convert_add_fusion.2 = f32[1024,768]{1,0:T(8,128)} fusion(bf16[1024,768]{1,0:T(8,128)(2,1)} %collective-permute-done.18, bf16[384,1024]{1,0:T(8,128)(2,1)S(1)} %get-tuple-element.192, bf16[384,1024]{1,0:T(8,128)(2,1)S(1)} %copy-done.49, bf16[384,768]{1,0:T(8,128)(2,1)S(1)} %copy-done.29, bf16[384,768]{1,0:T(8,128)(2,1)S(1)} %copy-done.24), kind=kOutput, calls=%fused_computation.3 | convolution fusion | flops 1215037440 | bytes 7471104 | tf_op jit(solution)/shard_map/dot_general | solution.py:18
  193.5 3.2 %fusion.23 = bf16[512,512]{1,0:T(8,128)(2,1)} fusion(bf16[1536,512]{1,0:T(8,128)(2,1)S(1)} %copy-done.2, bf16[1536,512]{1,0:T(8,128)(2,1)} %bitcast.13, f32[512]{0:T(512)S(1)} %copy-done.56), kind=kOutput, calls=%fused_computation.38 | convolution fusion | flops 805830656 | bytes 3672064 | tf_op jit(solution)/shard_map/dot_general | solution.py:18
  196.7 14.1 %all-to-all-done.2 = bf16[4,400,512]{2,1,0:T(8,128)(2,1)} async-done(((bf16[4,400,512]{2,1,0:T(8,128)(2,1)}), bf16[4,400,512]{2,1,0:T(8,128)(2,1)}, u32[]{:S(2)}, u32[]{:S(2)}) %all-to-all-start.2) | async-done | bytes 1638432 | tf_op jit(solution)/shard_map/all_to_all | solution.py:265
  (206 shorter events, 70.4 us)
Async XLA Ops:
  0.6 20.6 %collective-permute-start = (bf16[1024,768]{1,0:T(8,128)(2,1)}, bf16[1024,768]{1,0:T(8,128)(2,1)S(1)}, u32[]{:S(2)}, u32[]{:S(2)}) collective-permute-start(bf16[1024,768]{1,0:T(8,128)(2,1)} %gate.7), channel_id=1, source_target_pairs={{0,8},{8,0},{16,24},{24,16},{1,9},{9,1},{17,25},{25,17},{2,10},{10... | collective-permute-start | bytes 4718600 | tf_op jit(solution)/shard_map/ppermute | solution.py:97
  1.1 20.1 %collective-permute-start.1 = (bf16[1024,768]{1,0:T(8,128)(2,1)}, bf16[1024,768]{1,0:T(8,128)(2,1)}, u32[]{:S(2)}, u32[]{:S(2)}) collective-permute-start(bf16[1024,768]{1,0:T(8,128)(2,1)} %up.7), channel_id=1, source_target_pairs={{0,8},{8,0},{16,24},{24,16},{1,9},{9,1},{17,25},{25,17},{2,10},{10... | collective-permute-start | bytes 4718600 | tf_op jit(solution)/shard_map/ppermute | solution.py:97
  7.0 21.6 %collective-permute-start.2 = (bf16[384,1024]{1,0:T(8,128)(2,1)}, bf16[384,1024]{1,0:T(8,128)(2,1)}, u32[]{:S(2)}, u32[]{:S(2)}) collective-permute-start(bf16[384,1024]{1,0:T(8,128)(2,1)} %get-tuple-element.81), channel_id=1, source_target_pairs={{0,16},{8,24},{16,0},{24,8},{1,17},{9,25},{17,1},{25,9},{2,18},{10... | collective-permute-start | bytes 2359304 | tf_op jit(solution)/shard_map/ppermute | solution.py:97
  12.3 41.9 %all-to-all-start = ((bf16[4,384,512]{2,1,0:T(8,128)(2,1)}), bf16[4,384,512]{2,1,0:T(8,128)(2,1)}, u32[]{:S(2)}, u32[]{:S(2)}) async-start(bf16[4,384,512]{2,1,0:T(8,128)(2,1)} %bitcast.49), calls=%async_computation | async-start | bytes 3145728 | tf_op jit(solution)/shard_map/all_to_all | solution.py:265
  28.7 27.7 %collective-permute-start.4 = (bf16[384,1536]{1,0:T(8,128)(2,1)}, bf16[384,1536]{1,0:T(8,128)(2,1)}, u32[]{:S(2)}, u32[]{:S(2)}) collective-permute-start(bf16[384,1536]{1,0:T(8,128)(2,1)} %get-tuple-element.88), channel_id=1, source_target_pairs={{0,16},{8,24},{16,0},{24,8},{1,17},{9,25},{17,1},{25,9},{2,18},{10... | collective-permute-start | bytes 3538952 | tf_op jit(solution)/shard_map/ppermute | solution.py:97
  29.8 27.5 %collective-permute-start.3 = (bf16[384,1024]{1,0:T(8,128)(2,1)}, bf16[384,1024]{1,0:T(8,128)(2,1)}, u32[]{:S(2)}, u32[]{:S(2)}) collective-permute-start(bf16[384,1024]{1,0:T(8,128)(2,1)} %collective-permute-done.2.first.got), channel_id=1, source_target_pairs={{0,1},{1,0},{2,3},{3,2},{4,5},{5,4},{6,7},{7,6},{8,9},{9,8},{10,11... | collective-permute-start | bytes 2359304 | tf_op jit(solution)/shard_map/ppermute | solution.py:97
  31.3 44.0 %collective-permute-start.7 = (bf16[768,1024]{1,0:T(8,128)(2,1)S(1)}, bf16[768,1024]{1,0:T(8,128)(2,1)S(1)}, u32[]{:S(2)}, u32[]{:S(2)}) collective-permute-start(bf16[768,1024]{1,0:T(8,128)(2,1)S(1)} %copy-done), channel_id=1, source_target_pairs={{0,8},{8,0},{16,24},{24,16},{1,9},{9,1},{17,25},{25,17},{2,10},{10... | collective-permute-start | bytes 4718600 | tf_op jit(solution)/shard_map/ppermute | solution.py:97
  56.4 18.1 %collective-permute-start.5 = (bf16[384,1024]{1,0:T(8,128)(2,1)S(1)}, bf16[384,1024]{1,0:T(8,128)(2,1)S(1)}, u32[]{:S(2)}, u32[]{:S(2)}) collective-permute-start(bf16[384,1024]{1,0:T(8,128)(2,1)S(1)} %pad_maximum_fusion.4), channel_id=1, source_target_pairs={{0,16},{8,24},{16,0},{24,8},{1,17},{9,25},{17,1},{25,9},{2,18},{10... | collective-permute-start | bytes 2359304 | tf_op jit(solution)/shard_map/ppermute | solution.py:97
  57.4 19.5 %collective-permute-start.8 = (bf16[384,1024]{1,0:T(8,128)(2,1)S(1)}, bf16[384,1024]{1,0:T(8,128)(2,1)S(1)}, u32[]{:S(2)}, u32[]{:S(2)}) collective-permute-start(bf16[384,1024]{1,0:T(8,128)(2,1)S(1)} %pad_maximum_fusion.5.mine), channel_id=1, source_target_pairs={{0,1},{1,0},{2,3},{3,2},{4,5},{5,4},{6,7},{7,6},{8,9},{9,8},{10,11... | collective-permute-start | bytes 2359304 | tf_op jit(solution)/shard_map/ppermute | solution.py:97
  74.5 25.9 %collective-permute-start.6 = (bf16[384,1536]{1,0:T(8,128)(2,1)S(1)}, bf16[384,1536]{1,0:T(8,128)(2,1)S(1)}, u32[]{:S(2)}, u32[]{:S(2)}) collective-permute-start(bf16[384,1536]{1,0:T(8,128)(2,1)S(1)} %get-tuple-element.90), channel_id=1, source_target_pairs={{0,16},{8,24},{16,0},{24,8},{1,17},{9,25},{17,1},{25,9},{2,18},{10... | collective-permute-start | bytes 3538952 | tf_op jit(solution)/shard_map/ppermute | solution.py:97
  76.8 17.8 %collective-permute-start.9 = (bf16[384,1024]{1,0:T(8,128)(2,1)S(1)}, bf16[384,1024]{1,0:T(8,128)(2,1)S(1)}, u32[]{:S(2)}, u32[]{:S(2)}) collective-permute-start(bf16[384,1024]{1,0:T(8,128)(2,1)S(1)} %get-tuple-element.96), channel_id=1, source_target_pairs={{0,1},{1,0},{2,3},{3,2},{4,5},{5,4},{6,7},{7,6},{8,9},{9,8},{10,11... | collective-permute-start | bytes 2359304 | tf_op jit(solution)/shard_map/ppermute | solution.py:97
  94.6 16.5 %collective-permute-start.10 = (bf16[384,1024]{1,0:T(8,128)(2,1)S(1)}, bf16[384,1024]{1,0:T(8,128)(2,1)S(1)}, u32[]{:S(2)}, u32[]{:S(2)}) collective-permute-start(bf16[384,1024]{1,0:T(8,128)(2,1)S(1)} %collective-permute-done.5.mine.mine_rem), channel_id=1, source_target_pairs={{0,1},{1,0},{2,3},{3,2},{4,5},{5,4},{6,7},{7,6},{8,9},{9,8},{10,11... | collective-permute-start | bytes 2359304 | tf_op jit(solution)/shard_map/ppermute | solution.py:97
  100.4 13.5 %collective-permute-start.12 = (bf16[384,768]{1,0:T(8,128)(2,1)}, bf16[384,768]{1,0:T(8,128)(2,1)}, u32[]{:S(2)}, u32[]{:S(2)}) collective-permute-start(bf16[384,768]{1,0:T(8,128)(2,1)} %get-tuple-element.102), channel_id=1, source_target_pairs={{0,16},{8,24},{16,0},{24,8},{1,17},{9,25},{17,1},{25,9},{2,18},{10... | collective-permute-start | bytes 1769480 | tf_op jit(solution)/shard_map/ppermute | solution.py:97
  112.0 17.7 %collective-permute-start.11 = (bf16[384,1024]{1,0:T(8,128)(2,1)}, bf16[384,1024]{1,0:T(8,128)(2,1)}, u32[]{:S(2)}, u32[]{:S(2)}) collective-permute-start(bf16[384,1024]{1,0:T(8,128)(2,1)} %get-tuple-element.98), channel_id=1, source_target_pairs={{0,1},{1,0},{2,3},{3,2},{4,5},{5,4},{6,7},{7,6},{8,9},{9,8},{10,11... | collective-permute-start | bytes 2359304 | tf_op jit(solution)/shard_map/ppermute | solution.py:97
  113.9 18.8 %collective-permute-start.13 = (bf16[384,1024]{1,0:T(8,128)(2,1)}, bf16[384,1024]{1,0:T(8,128)(2,1)S(1)}, u32[]{:S(2)}, u32[]{:S(2)}) collective-permute-start(bf16[384,1024]{1,0:T(8,128)(2,1)} %add_convert_fusion.2), channel_id=1, source_target_pairs={{0,16},{8,24},{16,0},{24,8},{1,17},{9,25},{17,1},{25,9},{2,18},{10... | collective-permute-start | bytes 2359304 | tf_op jit(solution)/shard_map/ppermute | solution.py:97
  129.7 14.5 %collective-permute-start.15 = (bf16[384,1024]{1,0:T(8,128)(2,1)}, bf16[384,1024]{1,0:T(8,128)(2,1)}, u32[]{:S(2)}, u32[]{:S(2)}) collective-permute-start(bf16[384,1024]{1,0:T(8,128)(2,1)} %get-tuple-element.114), channel_id=1, source_target_pairs={{0,1},{1,0},{2,3},{3,2},{4,5},{5,4},{6,7},{7,6},{8,9},{9,8},{10,11... | collective-permute-start | bytes 2359304 | tf_op jit(solution)/shard_map/ppermute | solution.py:97
  132.7 13.2 %collective-permute-start.14 = (bf16[384,768]{1,0:T(8,128)(2,1)}, bf16[384,768]{1,0:T(8,128)(2,1)}, u32[]{:S(2)}, u32[]{:S(2)}) collective-permute-start(bf16[384,768]{1,0:T(8,128)(2,1)} %get-tuple-element.108), channel_id=1, source_target_pairs={{0,16},{8,24},{16,0},{24,8},{1,17},{9,25},{17,1},{25,9},{2,18},{10... | collective-permute-start | bytes 1769480 | tf_op jit(solution)/shard_map/ppermute | solution.py:97
  136.0 35.0 %all-to-all-start.1 = ((bf16[4,384,512]{2,1,0:T(8,128)(2,1)}), bf16[4,384,512]{2,1,0:T(8,128)(2,1)}, u32[]{:S(2)}, u32[]{:S(2)}) async-start(bf16[4,384,512]{2,1,0:T(8,128)(2,1)} %pad_maximum_fusion.2), calls=%async_computation.1 | async-start | bytes 3145728 | tf_op jit(solution)/shard_map/all_to_all | solution.py:265
  148.8 16.1 %collective-permute-start.17 = (bf16[384,1024]{1,0:T(8,128)(2,1)S(1)}, bf16[384,1024]{1,0:T(8,128)(2,1)S(1)}, u32[]{:S(2)}, u32[]{:S(2)}) collective-permute-start(bf16[384,1024]{1,0:T(8,128)(2,1)S(1)} %add_convert_fusion), channel_id=1, source_target_pairs={{0,16},{8,24},{16,0},{24,8},{1,17},{9,25},{17,1},{25,9},{2,18},{10... | collective-permute-start | bytes 2359304 | tf_op jit(solution)/shard_map/ppermute | solution.py:97
  154.9 14.0 %collective-permute-start.16 = (bf16[400,1024]{1,0:T(8,128)(2,1)S(1)}, bf16[400,1024]{1,0:T(8,128)(2,1)S(1)}, u32[]{:S(2)}, u32[]{:S(2)}) collective-permute-start(bf16[400,1024]{1,0:T(8,128)(2,1)S(1)} %fusion.37), channel_id=1, source_target_pairs={{0,1},{1,0},{2,3},{3,2},{4,5},{5,4},{6,7},{7,6},{8,9},{9,8},{10,11... | collective-permute-start | bytes 2457608 | tf_op jit(solution)/shard_map/ppermute | solution.py:97
  164.3 13.0 %collective-permute-start.20 = (bf16[768,1024]{1,0:T(8,128)(2,1)}, bf16[768,1024]{1,0:T(8,128)(2,1)}, u32[]{:S(2)}, u32[]{:S(2)}) collective-permute-start(bf16[768,1024]{1,0:T(8,128)(2,1)} %get-tuple-element.149), channel_id=1, source_target_pairs={{0,8},{8,0},{16,24},{24,16},{1,9},{9,1},{17,25},{25,17},{2,10},{10... | collective-permute-start | bytes 4718600 | tf_op jit(solution)/shard_map/ppermute | solution.py:97
  164.3 19.8 %collective-permute-start.19 = (bf16[1024,768]{1,0:T(8,128)(2,1)}, bf16[1024,768]{1,0:T(8,128)(2,1)}, u32[]{:S(2)}, u32[]{:S(2)}) collective-permute-start(bf16[1024,768]{1,0:T(8,128)(2,1)} %get-tuple-element.142), channel_id=1, source_target_pairs={{0,8},{8,0},{16,24},{24,16},{1,9},{9,1},{17,25},{25,17},{2,10},{10... | collective-permute-start | bytes 4718600 | tf_op jit(solution)/shard_map/ppermute | solution.py:97
  164.8 23.9 %collective-permute-start.18 = (bf16[1024,768]{1,0:T(8,128)(2,1)S(1)}, bf16[1024,768]{1,0:T(8,128)(2,1)}, u32[]{:S(2)}, u32[]{:S(2)}) collective-permute-start(bf16[1024,768]{1,0:T(8,128)(2,1)S(1)} %get-tuple-element.136), channel_id=1, source_target_pairs={{0,8},{8,0},{16,24},{24,16},{1,9},{9,1},{17,25},{25,17},{2,10},{10... | collective-permute-start | bytes 4718600 | tf_op jit(solution)/shard_map/ppermute | solution.py:97
  171.0 39.7 %all-to-all-start.2 = ((bf16[4,400,512]{2,1,0:T(8,128)(2,1)}), bf16[4,400,512]{2,1,0:T(8,128)(2,1)}, u32[]{:S(2)}, u32[]{:S(2)}) async-start(bf16[4,400,512]{2,1,0:T(8,128)(2,1)} %pad_maximum_fusion), calls=%async_computation.2 | async-start | bytes 3276800 | tf_op jit(solution)/shard_map/all_to_all | solution.py:265
  (59 other events, 305.1 us)
